TPU v7x, 32 devices: a whole 2x2x4 slice. The times are simulated.
32 devices in a mesh: rep: 8 (over z, x), cp: 4 (over y, core).
Axes of the slice: x: 2, y: 2, z: 4, core: 2. Of those that a mesh axis runs over, the one named last changes fastest.
Arguments:
- tokens: bfloat16 [8192, 768], P(('rep', 'cp')), may hold values from -6 to 6
- cotangent: bfloat16 [8192, 768], P(('rep', 'cp')), may hold values from -6 to 6
- ln1_gain: bfloat16 [768], P('cp'), may hold values from 0.099609375 to 1.8984375
- ln1_bias: bfloat16 [768], P('cp'), may hold values from -3 to 3
- w_qkv: bfloat16 [768, 2304], P('cp'), may hold values from -0.21875 to 0.21875
- b_qv: bfloat16 [1536], P('cp'), may hold values from -3 to 3
- w_out: bfloat16 [768, 768], P('cp'), may hold values from -3 to 3
- b_out: bfloat16 [768], P('cp'), may hold values from -3 to 3
- ln2_gain: bfloat16 [768], P('cp'), may hold values from 0.099609375 to 1.8984375
- ln2_bias: bfloat16 [768], P('cp'), may hold values from -3 to 3
- w_in: bfloat16 [768, 3072], P('cp'), may hold values from -0.21875 to 0.21875
- b_in: bfloat16 [3072], P('cp'), may hold values from -3 to 3
- w_down: bfloat16 [3072, 768], P('cp'), may hold values from -0.109375 to 0.109375
- b_down: bfloat16 [768], P('cp'), may hold values from -3 to 3
Outputs:
- layer_out: bfloat16 [8192, 768], P(('rep', 'cp'))
- input_grad: bfloat16 [8192, 768], P(('rep', 'cp'))
- grad_ln1_gain: float32 [768], P('cp')
- grad_ln1_bias: float32 [768], P('cp')
- grad_w_qkv: float32 [768, 2304], P('cp')
- grad_b_qv: float32 [1536], P('cp')
- grad_w_out: float32 [768, 768], P('cp')
- grad_b_out: float32 [768], P('cp')
- grad_ln2_gain: float32 [768], P('cp')
- grad_ln2_bias: float32 [768], P('cp')
- grad_w_in: float32 [768, 3072], P('cp')
- grad_b_in: float32 [3072], P('cp')
- grad_w_down: float32 [3072, 768], P('cp')
- grad_b_down: float32 [768], P('cp')
All inputs are finite; a program needn't handle non-finite values.
Results may differ from a plain program's by a relative error of at most 0.011.
Values may be sent and summed in bfloat16 or wider, within the bound.
A program may use at most 192 MiB of HBM per device.

v0:
```python
from functools import partial

import jax
import jax.numpy as jnp
from jax import lax
from jax.sharding import PartitionSpec as P

D = 768
H = 12
HD = 64


def layer_norm(values, gain, shift):
    centred = values - jnp.mean(values, axis=-1, keepdims=True)
    variance = jnp.mean(centred * centred, axis=-1, keepdims=True)
    return centred * lax.rsqrt(variance + 1e-05) * gain + shift


def along_rows(left, right):
    return lax.dot_general(
        left, right, (((1,), (1,)), ((), ())), preferred_element_type=jnp.float32
    )


def across_rows(left, right):
    return lax.dot_general(
        left, right, (((0,), (0,)), ((), ())), preferred_element_type=jnp.float32
    )


def body(
    tokens,
    cotangent,
    ln1_gain,
    ln1_bias,
    w_qkv,
    b_qv,
    w_out,
    b_out,
    ln2_gain,
    ln2_bias,
    w_in,
    b_in,
    w_down,
    b_down,
):
    (
        gain_one,
        shift_one,
        qkv_full,
        qv_bias,
        out_full,
        out_bias,
        gain_two,
        shift_two,
        in_full,
        in_bias,
        down_full,
        down_bias,
    ) = (
        lax.all_gather(ln1_gain, "cp", axis=0, tiled=True),
        lax.all_gather(ln1_bias, "cp", axis=0, tiled=True),
        lax.all_gather(w_qkv, "cp", axis=0, tiled=True),
        lax.all_gather(b_qv, "cp", axis=0, tiled=True),
        lax.all_gather(w_out, "cp", axis=0, tiled=True),
        lax.all_gather(b_out, "cp", axis=0, tiled=True),
        lax.all_gather(ln2_gain, "cp", axis=0, tiled=True),
        lax.all_gather(ln2_bias, "cp", axis=0, tiled=True),
        lax.all_gather(w_in, "cp", axis=0, tiled=True),
        lax.all_gather(b_in, "cp", axis=0, tiled=True),
        lax.all_gather(w_down, "cp", axis=0, tiled=True),
        lax.all_gather(b_down, "cp", axis=0, tiled=True),
    )
    token_rows = tokens.shape[0]
    first_row = lax.axis_index("cp") * token_rows
    scale = HD ** (-0.5)
    query_places = first_row + jnp.arange(token_rows, dtype=jnp.int32)

    def allowed_mask(count):
        return (query_places[:, None] >= jnp.arange(count, dtype=jnp.int32)[None, :])[None]

    inputs = tokens.astype(jnp.float32)
    normed, norm_one_back = jax.vjp(
        layer_norm, inputs, gain_one.astype(jnp.float32), shift_one.astype(jnp.float32)
    )
    normed_low = normed.astype(jnp.bfloat16)
    mixed = jnp.dot(normed_low, qkv_full, preferred_element_type=jnp.float32)
    bias_float = qv_bias.astype(jnp.float32)
    query = (mixed[:, :D] + bias_float[:D]).astype(jnp.bfloat16)
    keys = mixed[:, D : 2 * D].astype(jnp.bfloat16)
    values = (mixed[:, 2 * D :] + bias_float[D:]).astype(jnp.bfloat16)
    query_heads = query.reshape(token_rows, H, HD)
    weighted = jnp.zeros((token_rows, H, HD), jnp.float32)
    running_top = jnp.full((H, token_rows), -1e30, jnp.float32)
    key_piece = lax.all_gather(keys, "cp", axis=0, tiled=True)
    value_piece = lax.all_gather(values, "cp", axis=0, tiled=True)
    count = key_piece.shape[0]
    key_heads = key_piece.reshape(count, H, HD)
    value_heads = value_piece.astype(jnp.float32).reshape(count, H, HD)
    allowed = allowed_mask(count)
    scores = (
        jnp.einsum("qhd,khd->hqk", query_heads, key_heads, preferred_element_type=jnp.float32)
        * scale
    )
    scores = jnp.where(allowed, scores, -1e30)
    new_top = jnp.maximum(running_top, jnp.max(scores, axis=-1))
    factor = jnp.exp(running_top - new_top)
    probs = jnp.where(allowed, jnp.exp(scores - new_top[..., None]), 0.0)
    running_total = jnp.sum(probs, axis=-1)
    update = jnp.einsum("hqk,khd->qhd", probs, value_heads, precision=lax.Precision.HIGHEST)
    weighted = weighted * factor.T[..., None] + update
    weighted, running_top, running_total = (weighted, new_top, running_total)
    out_exact = weighted / running_total.T[..., None]
    logsum = running_top + jnp.log(running_total)
    attended_low = out_exact.reshape(token_rows, D).astype(jnp.bfloat16)
    middle = inputs + (
        jnp.dot(attended_low, out_full, preferred_element_type=jnp.float32)
        + out_bias.astype(jnp.float32)
    )
    normed_two, norm_two_back = jax.vjp(
        layer_norm, middle, gain_two.astype(jnp.float32), shift_two.astype(jnp.float32)
    )
    normed_two_low = normed_two.astype(jnp.bfloat16)
    hidden = jnp.dot(normed_two_low, in_full, preferred_element_type=jnp.float32) + in_bias.astype(
        jnp.float32
    )
    active, gelu_back = jax.vjp(partial(jax.nn.gelu, approximate=True), hidden)
    active_low = active.astype(jnp.bfloat16)
    result = (
        middle
        + jnp.dot(active_low, down_full, preferred_element_type=jnp.float32)
        + down_bias.astype(jnp.float32)
    )
    layer_out = result.astype(jnp.bfloat16)
    qkv_back, out_back, in_back, down_back = (
        lax.all_gather(w_qkv, "cp", axis=0, tiled=True),
        lax.all_gather(w_out, "cp", axis=0, tiled=True),
        lax.all_gather(w_in, "cp", axis=0, tiled=True),
        lax.all_gather(w_down, "cp", axis=0, tiled=True),
    )
    grad_output = cotangent.astype(jnp.float32)
    grad_down = across_rows(active_low, cotangent)
    grad_down_bias = jnp.sum(grad_output, axis=0)
    grad_active = along_rows(cotangent, down_back)
    grad_hidden = gelu_back(grad_active)[0].astype(jnp.bfloat16)
    grad_in = across_rows(normed_two_low, grad_hidden)
    grad_in_bias = jnp.sum(grad_hidden.astype(jnp.float32), axis=0)
    grad_middle_part, grad_gain_two, grad_shift_two = norm_two_back(
        along_rows(grad_hidden, in_back)
    )
    grad_middle = grad_output + grad_middle_part
    grad_branch = grad_middle.astype(jnp.bfloat16)
    grad_out_proj = across_rows(attended_low, grad_branch)
    grad_out_bias = jnp.sum(grad_branch.astype(jnp.float32), axis=0)
    grad_attended = along_rows(grad_branch, out_back).astype(jnp.bfloat16)
    grad_heads = grad_attended.reshape(token_rows, H, HD)
    grad_heads_float = grad_heads.astype(jnp.float32)
    delta = jnp.einsum("qhd,qhd->hq", grad_heads_float, out_exact)
    key_piece = lax.all_gather(keys, "cp", axis=0, tiled=True)
    value_piece = lax.all_gather(values, "cp", axis=0, tiled=True)
    count = key_piece.shape[0]
    key_heads = key_piece.reshape(count, H, HD)
    value_heads = value_piece.reshape(count, H, HD)
    allowed = allowed_mask(count)
    scores = (
        jnp.einsum("qhd,khd->hqk", query_heads, key_heads, preferred_element_type=jnp.float32)
        * scale
    )
    probs = jnp.where(allowed, jnp.exp(scores - logsum[..., None]), 0.0)
    grad_probs = jnp.einsum(
        "qhd,khd->hqk", grad_heads, value_heads, preferred_element_type=jnp.float32
    )
    grad_scores = (probs * (grad_probs - delta[..., None])).astype(jnp.bfloat16)
    grad_query = jnp.einsum(
        "hqk,khd->qhd", grad_scores, key_heads, preferred_element_type=jnp.float32
    )
    paired = jnp.concatenate([keys, values], axis=1)
    piece = lax.all_gather(paired, "cp", axis=0, tiled=True)
    count = piece.shape[0]
    key_heads = piece[:, :D].reshape(count, H, HD)
    value_heads = piece[:, D:].reshape(count, H, HD)
    allowed = allowed_mask(count)
    scores = (
        jnp.einsum("qhd,khd->hqk", query_heads, key_heads, preferred_element_type=jnp.float32)
        * scale
    )
    probs = jnp.where(allowed, jnp.exp(scores - logsum[..., None]), 0.0)
    grad_probs = jnp.einsum(
        "qhd,khd->hqk", grad_heads, value_heads, preferred_element_type=jnp.float32
    )
    grad_scores = (probs * (grad_probs - delta[..., None])).astype(jnp.bfloat16)
    key_term = (
        jnp.einsum(
            "hqk,qhd->khd", grad_scores, query_heads, preferred_element_type=jnp.float32
        ).reshape(count, D)
        * scale
    )
    value_term = jnp.einsum(
        "hqk,qhd->khd", probs, grad_heads_float, precision=lax.Precision.HIGHEST
    ).reshape(count, D)
    terms = jnp.concatenate([key_term, value_term], axis=1)
    owned_terms = lax.psum_scatter(terms, "cp", scatter_dimension=0, tiled=True)
    grad_keys = owned_terms[:, :D]
    grad_values = owned_terms[:, D:]
    grad_query_low = (grad_query * scale).reshape(token_rows, D).astype(jnp.bfloat16)
    grad_mixed = jnp.concatenate(
        [grad_query_low, grad_keys.astype(jnp.bfloat16), grad_values.astype(jnp.bfloat16)], axis=1
    )
    grad_qkv = across_rows(normed_low, grad_mixed)
    mixed_sums = jnp.sum(grad_mixed.astype(jnp.float32), axis=0)
    grad_qv_bias = jnp.concatenate([mixed_sums[:D], mixed_sums[2 * D :]])
    grad_input_part, grad_gain_one, grad_shift_one = norm_one_back(along_rows(grad_mixed, qkv_back))
    input_grad = (grad_middle + grad_input_part).astype(jnp.bfloat16)
    owned = (
        lax.psum_scatter(grad_gain_one, "cp", scatter_dimension=0, tiled=True),
        lax.psum_scatter(grad_shift_one, "cp", scatter_dimension=0, tiled=True),
        lax.psum_scatter(grad_qkv, "cp", scatter_dimension=0, tiled=True),
        lax.psum_scatter(grad_qv_bias, "cp", scatter_dimension=0, tiled=True),
        lax.psum_scatter(grad_out_proj, "cp", scatter_dimension=0, tiled=True),
        lax.psum_scatter(grad_out_bias, "cp", scatter_dimension=0, tiled=True),
        lax.psum_scatter(grad_gain_two, "cp", scatter_dimension=0, tiled=True),
        lax.psum_scatter(grad_shift_two, "cp", scatter_dimension=0, tiled=True),
        lax.psum_scatter(grad_in, "cp", scatter_dimension=0, tiled=True),
        lax.psum_scatter(grad_in_bias, "cp", scatter_dimension=0, tiled=True),
        lax.psum_scatter(grad_down, "cp", scatter_dimension=0, tiled=True),
        lax.psum_scatter(grad_down_bias, "cp", scatter_dimension=0, tiled=True),
    )
    totals = lax.psum(
        (
            owned[0],
            owned[1],
            owned[2],
            owned[3],
            owned[4],
            owned[5],
            owned[6],
            owned[7],
            owned[8],
            owned[9],
            owned[10],
            owned[11],
        ),
        "rep",
    )
    return (layer_out, input_grad) + tuple(totals)


def solution(mesh):
    placed = (
        P(("rep", "cp"), None),
        P(("rep", "cp"), None),
        P("cp"),
        P("cp"),
        P("cp", None),
        P("cp"),
        P("cp", None),
        P("cp"),
        P("cp"),
        P("cp"),
        P("cp", None),
        P("cp"),
        P("cp", None),
        P("cp"),
    )
    return jax.shard_map(
        body,
        mesh=mesh,
        in_specs=placed,
        out_specs=(
            P(("rep", "cp"), None),
            P(("rep", "cp"), None),
            P("cp"),
            P("cp"),
            P("cp", None),
            P("cp"),
            P("cp", None),
            P("cp"),
            P("cp"),
            P("cp"),
            P("cp", None),
            P("cp"),
            P("cp", None),
            P("cp"),
        ),
        check_vma=False,
    )
```

profile of v0, /device:TPU:0, one launch (start us, length us, event | category | flops | bytes accessed | tf_op | source)
XLA Modules:
  0.0 838.7 jit_solution(10062626976144416109)
XLA Ops:
  15.7 13.7 %all-reduce.17 = (bf16[768]{0:T(1024)(128)(2,1)S(1)}, bf16[768]{0:T(1024)(128)(2,1)S(1)}, bf16[768]{0:T(1024)(128)(2,1)S(1)}, bf16[768]{0:T(1024)(128)(2,1)}, bf...) all-reduce(bf16[768]{0:T(1024)(128)(2,1)S(1)} %dynamic-update-slice.1, ...), channel_id=1, replica_groups=mesh['rep'=8,'cp'=4] {'cp'}, use_global_device_ids=true, to_apply=%add.1 | all-reduce | flops 4608 | bytes 18432
  31.9 11.4 %all-gather.10.cloned.1.call-done = bf16[768,2304]{1,0:T(8,128)(2,1)} async-done(((bf16[192,2304]{1,0:T(8,128)(2,1)}), bf16[768,2304]{1,0:T(8,128)(2,1)}) %all-gather.10.cloned.1.call-update) | async-done | bytes 3538960 | tf_op jit(solution)/shard_map/all_gather | solution.py:63
  61.8 20.7 %all-gather.20.cloned.1.call-done = bf16[3072,768]{1,0:T(8,128)(2,1)} async-done(((bf16[768,768]{1,0:T(8,128)(2,1)}), bf16[3072,768]{1,0:T(8,128)(2,1)}) %all-gather.20.cloned.1.call-update) | async-done | bytes 4718608 | tf_op jit(solution)/shard_map/all_gather | solution.py:71
  87.8 16.4 %all-gather.12.cloned.1.call-done = bf16[1024,768]{1,0:T(8,128)(2,1)} async-done(((bf16[256,768]{1,0:T(8,128)(2,1)}), bf16[1024,768]{1,0:T(8,128)(2,1)}) %all-gather.12.cloned.1.call-update) | async-done | bytes 1572880 | tf_op jit(solution)/shard_map/all_gather | solution.py:95
  113.7 12.3 %all-gather.14.cloned.1.call-done = bf16[1024,768]{1,0:T(8,128)(2,1)} async-done(((bf16[256,768]{1,0:T(8,128)(2,1)}), bf16[1024,768]{1,0:T(8,128)(2,1)}) %all-gather.14.cloned.1.call-update) | async-done | bytes 1572880 | tf_op jit(solution)/shard_map/all_gather | solution.py:96
  127.7 13.7 %fusion.79 = (bf16[256,12,64]{0,2,1:T(8,128)(2,1)S(1)}, f32[256,12,64]{0,2,1:T(8,128)}) fusion(f32[256,12]{0,1:T(8,128)S(1)} %bitcast.82, bf16[1024,12,64]{0,2,1:T(8,128)(2,1)S(1)} %bitcast.72, f32[12,256,1024]{2,1,0:T(8,128)} %copy-done, f32[12,256]{1,0:T(8,128)S(1)} %broadcast_maximum_fusion, pred[256,1024]{1,0:T(8,128)(4,1)S(1)} %iota_compare_fusion, ...), kind=kOutput, calls=%fused_computation.122 | convolution fusion | flops 2429091840 | bytes 15634432 | tf_op jit(solution)/shard_map/hqk,khd->qhd/dot_general | solution.py:110
  147.0 36.8 %all-gather.18.cloned.1.call-done = bf16[768,3072]{1,0:T(8,128)(2,1)} async-done(((bf16[192,3072]{1,0:T(8,128)(2,1)}), bf16[768,3072]{1,0:T(8,128)(2,1)}) %all-gather.18.cloned.1.call-update) | async-done | bytes 4718608 | tf_op jit(solution)/shard_map/all_gather | solution.py:69
  183.8 9.0 %convert_reduce_fusion = (f32[3072]{0:T(1024)}, bf16[256,3072]{1,0:T(8,128)(2,1)S(1)}, f32[256,3072]{1,0:T(8,128)}) fusion(f32[256,3072]{1,0:T(8,128)} %fusion.81, f32[3072]{0:T(1024)S(1)} %bitcast.83, bf16[768,3072]{1,0:T(8,128)(2,1)} %all-gather.18.cloned.1.call-done, f32[256,768]{1,0:T(8,128)S(1)} %get-tuple-element.72, ...), kind=kOutput, calls=%fused_computation.34 | convolution fusion | flops 1227027456 | bytes 13402112 | tf_op jit(solution)/shard_map/dot_general | solution.py:124
  199.1 15.4 %all-gather.22.cloned.1.call-done = bf16[1024,1536]{1,0:T(8,128)(2,1)} async-done(((bf16[256,1536]{1,0:T(8,128)(2,1)}), bf16[1024,1536]{1,0:T(8,128)(2,1)}) %all-gather.22.cloned.1.call-update) | async-done | bytes 3145744 | tf_op jit(solution)/shard_map/all_gather | solution.py:178
  219.9 7.3 fusion.82
  229.9 12.3 %fusion = f32[12,64,1024]{2,1,0:T(8,128)} fusion(bf16[256,12,64]{0,2,1:T(8,128)(2,1)S(1)} %bitcast.76, f32[12,256,1024]{2,1,0:T(8,128)} %fusion.82, f32[12,256]{1,0:T(8,128)S(1)} %copy-done.33, pred[256,1024]{1,0:T(8,128)(4,1)S(1)} %copy-done.13), kind=kOutput, calls=%fused_computation.5 | convolution fusion | flops 2425356288 | bytes 16396288 | tf_op jit(solution)/shard_map/hqk,qhd->khd/dot_general | solution.py:198
  242.2 12.1 %fusion.27 = f32[12,64,1024]{2,1,0:T(8,128)} fusion(bf16[256,12,64]{0,2,1:T(8,128)(2,1)S(1)} %bitcast.67, f32[12,256,1024]{2,1,0:T(8,128)} %fusion.82, f32[12,256]{1,0:T(8,128)S(1)} %copy-done.31, f32[12,256]{1,0:T(8,128)S(1)} %copy-done.33, pred[256,1024]{1,0:T(8,128)(4,1)S(1)} %copy-done.13, bf16[256,12,64]{0,2,1:T(8,128)(2,1)S(1)} %bitcast.77, ...), kind=kOutput, calls=%fused_computation.37 | convolution fusion | flops 824967168 | bytes 18374656 | tf_op jit(solution)/shard_map/hqk,qhd->khd/dot_general | solution.py:193
  254.4 6.7 pad_maximum_fusion
  264.1 7.8 fusion.70
  273.0 7.9 fusion.71
  281.2 12.8 %fusion.33 = bf16[12,64,256]{2,1,0:T(8,128)(2,1)} fusion(bf16[1024,12,64]{0,2,1:T(8,128)(2,1)} %bitcast.64, f32[12,256,1024]{2,1,0:T(8,128)} %copy-done, f32[12,256]{1,0:T(8,128)S(1)} %copy-done.31, f32[12,256]{1,0:T(8,128)S(1)} %copy-done.33, pred[256,1024]{1,0:T(8,128)(4,1)S(1)} %copy-done.13, bf16[256,12,64]{0,2,1:T(8,128)(2,1)S(1)} %bitcast.78, ...), kind=kOutput, calls=%fused_computation.45 | convolution fusion | flops 824573952 | bytes 16801792 | tf_op jit(solution)/shard_map/hqk,khd->qhd/dot_general | solution.py:174
  294.0 25.7 %reduce-scatter.6.cloned.1.call-done = f32[256,1536]{0,1:T(8,128)} async-done(((f32[1024,1536]{0,1:T(8,128)}), f32[256,1536]{0,1:T(8,128)}) %reduce-scatter.6.cloned.1.call-update) | async-done | bytes 1572880 | tf_op jit(solution)/shard_map/reduce_scatter | solution.py:202
  326.4 29.6 %reduce-scatter.10.cloned.1.call-done = f32[192,768]{1,0:T(8,128)} async-done(((f32[768,768]{1,0:T(8,128)}), f32[192,768]{1,0:T(8,128)}) %reduce-scatter.10.cloned.1.call-update) | async-done | bytes 589840 | tf_op jit(solution)/shard_map/reduce_scatter | solution.py:219
  356.0 80.8 %reduce-scatter.12.cloned.1.call-done = f32[192,3072]{1,0:T(8,128)} async-done(((f32[768,3072]{1,0:T(8,128)}), f32[192,3072]{1,0:T(8,128)}) %reduce-scatter.12.cloned.1.call-update) | async-done | bytes 2359312 | tf_op jit(solution)/shard_map/reduce_scatter | solution.py:223
  436.8 81.0 %reduce-scatter.14.cloned.1.call-done = f32[768,768]{1,0:T(8,128)} async-done(((f32[3072,768]{1,0:T(8,128)}), f32[768,768]{1,0:T(8,128)}) %reduce-scatter.14.cloned.1.call-update) | async-done | bytes 2359312 | tf_op jit(solution)/shard_map/reduce_scatter | solution.py:225
  517.8 66.1 %reduce-scatter.8.cloned.1.call-done = f32[192,2304]{1,0:T(8,128)} async-done(((f32[768,2304]{1,0:T(8,128)}), f32[192,2304]{1,0:T(8,128)}) %reduce-scatter.8.cloned.1.call-update) | async-done | bytes 1769488 | tf_op jit(solution)/shard_map/reduce_scatter | solution.py:217
  595.9 11.4 %all-reduce.16 = (f32[768]{0:T(1024)S(1)}, f32[768]{0:T(1024)S(1)}, f32[1536]{0:T(1024)S(1)}, f32[768]{0:T(1024)S(1)}, f32[768]{0:T(1024)S(1)}, /*index=5*/f32[7...) all-reduce(f32[768]{0:T(1024)S(1)} %get-tuple-element.16, ...), channel_id=3, replica_groups=mesh['rep'=8,'cp'=4] {'cp'}, use_global_device_ids=true, to_apply=%region_12.13.clone | all-reduce | flops 9216 | bytes 73728
  607.8 39.2 %all-reduce.14 = (f32[192]{0:T(256)}, f32[192]{0:T(256)}, f32[384]{0:T(512)}, f32[192]{0:T(256)}, f32[192]{0:T(256)}, /*index=5*/f32[192]{0:T(256)}, f32[768]{0:T(1024)}, f32[192]{0:T(256)}) all-reduce(f32[192]{0:T(256)S(1)} %dynamic-slice.7, f32[192]{0:T(256)S(1)} %dynamic-slice.9, ...), channel_id=1, replica_groups=mesh['rep'=8,'cp'=4] {'rep'}, use_global_device_ids=true, to_apply=%region_13.14 | all-reduce | flops 2304 | bytes 18432 | tf_op jit(solution)/shard_map/psum | solution.py:228
  647.0 178.3 %all-reduce.20.cloned.1.call-done = (f32[192,2304]{1,0:T(8,128)}, f32[192,768]{1,0:T(8,128)}, f32[192,3072]{1,0:T(8,128)}, f32[768,768]{1,0:T(8,128)}) async-done(((f32[192,2304]{1,0:T(8,128)}, f32[192,768]{1,0:T(8,128)}, f32[192,3072]{1,0:T(8,128)}, f32[768,768]{1,0:T(8,128)}), (f32[192,2304]{1,0:T(8,128)}, f32[192,768]{1,0:T(8,128)}, f32[192,3072]{1,0:T(8,128)}, ...) | async-done | bytes 7077904 | tf_op jit(solution)/shard_map/psum | solution.py:228
  (208 shorter events, 93.1 us)
Async XLA Ops:
  7.2 36.1 %all-gather.10.cloned.1.call-start = ((), (), s32[]{:S(2)}) async-start(), calls=%async_computation.5 | async-start | bytes 4423680 | tf_op jit(solution)/shard_map/all_gather | solution.py:63
  7.9 74.5 %all-gather.20.cloned.1.call-start = ((), (), s32[]{:S(2)}) async-start(), calls=%async_computation.10 | async-start | bytes 5898240 | tf_op jit(solution)/shard_map/all_gather | solution.py:71
  8.7 95.6 %all-gather.12.cloned.1.call-start = ((), (), s32[]{:S(2)}) async-start(), calls=%async_computation.6 | async-start | bytes 1966080 | tf_op jit(solution)/shard_map/all_gather | solution.py:95
  30.6 16.0 %copy-start.25 = (f32[256]{0:T(256)}, f32[256]{0:T(256)S(1)}, u32[]{:S(2)}) copy-start(f32[256]{0:T(256)S(1)} %broadcast_multiply_fusion.1) | copy-start | bytes 3076
  47.4 78.5 %all-gather.14.cloned.1.call-start = ((), (), s32[]{:S(2)}) async-start(), calls=%async_computation.7 | async-start | bytes 1966080 | tf_op jit(solution)/shard_map/all_gather | solution.py:96
  53.7 28.7 %copy-start.2 = (bf16[256,768]{1,0:T(8,128)(2,1)S(1)}, bf16[256,768]{1,0:T(8,128)(2,1)}, u32[]{:S(2)}) copy-start(bf16[256,768]{1,0:T(8,128)(2,1)} %param.15) | copy-start | bytes 1179652
  53.7 91.1 %all-gather.16.cloned.1.call-start = ((), (), s32[]{:S(2)}) async-start(), calls=%async_computation.8 | async-start | bytes 1474560 | tf_op jit(solution)/shard_map/all_gather | solution.py:65
  54.3 129.4 %all-gather.18.cloned.1.call-start = ((), (), s32[]{:S(2)}) async-start(), calls=%async_computation.9 | async-start | bytes 5898240 | tf_op jit(solution)/shard_map/all_gather | solution.py:69
  54.9 159.6 %all-gather.22.cloned.1.call-start = ((), (), s32[]{:S(2)}) async-start(), calls=%async_computation.11 | async-start | bytes 3932160 | tf_op jit(solution)/shard_map/all_gather | solution.py:178
  60.5 67.2 %copy-start.12 = (pred[256,1024]{1,0:T(8,128)(4,1)}, pred[256,1024]{1,0:T(8,128)(4,1)S(1)}, u32[]{:S(2)}) copy-start(pred[256,1024]{1,0:T(8,128)(4,1)S(1)} %iota_compare_fusion) | copy-start | bytes 786436
  60.7 45.5 %copy-start.10 = (bf16[256,768]{0,1:T(8,128)(2,1)}, bf16[256,768]{0,1:T(8,128)(2,1)S(1)}, u32[]{:S(2)}) copy-start(bf16[256,768]{0,1:T(8,128)(2,1)S(1)} %copy.42) | copy-start | bytes 1179652
  61.7 257.9 %reduce-scatter.6.cloned.1.call-start = ((), (), s32[]{:S(2)}) async-start(), calls=%async_computation.12 | async-start | bytes 7864320 | tf_op jit(solution)/shard_map/reduce_scatter | solution.py:202
  127.7 17.2 %copy-start.1 = (bf16[256,768]{1,0:T(8,128)(2,1)S(1)}, bf16[256,768]{1,0:T(8,128)(2,1)}, u32[]{:S(2)}) copy-start(bf16[256,768]{1,0:T(8,128)(2,1)} %param.14) | copy-start | bytes 1179652
  141.5 51.3 %copy-start.16 = (bf16[256,12,64]{0,2,1:T(8,128)(2,1)}, bf16[256,12,64]{0,2,1:T(8,128)(2,1)S(1)}, u32[]{:S(2)}) copy-start(bf16[256,12,64]{0,2,1:T(8,128)(2,1)S(1)} %get-tuple-element.69) | copy-start | bytes 1179652
  146.7 46.0 %copy-start.29 = (f32[256]{0:T(256)}, f32[256]{0:T(256)S(1)}, u32[]{:S(2)}) copy-start(f32[256]{0:T(256)S(1)} %broadcast_multiply_fusion) | copy-start | bytes 3076
  147.0 45.8 %copy-start.34 = (f32[256]{0:T(256)}, f32[256]{0:T(256)S(1)}, u32[]{:S(2)}) copy-start(f32[256]{0:T(256)S(1)} %fusion.54) | copy-start | bytes 3076
  198.4 19.9 %copy-start.19 = (bf16[256,768]{0,1:T(8,128)(2,1)}, bf16[256,768]{0,1:T(8,128)(2,1)S(1)}, u32[]{:S(2)}) copy-start(bf16[256,768]{0,1:T(8,128)(2,1)S(1)} %copy.45) | copy-start | bytes 1179652
  261.1 94.9 %reduce-scatter.10.cloned.1.call-start = ((), (), s32[]{:S(2)}) async-start(), calls=%async_computation.14 | async-start | bytes 2949120 | tf_op jit(solution)/shard_map/reduce_scatter | solution.py:219
  264.1 172.7 %reduce-scatter.12.cloned.1.call-start = ((), (), s32[]{:S(2)}) async-start(), calls=%async_computation.15 | async-start | bytes 11796480 | tf_op jit(solution)/shard_map/reduce_scatter | solution.py:223
  272.0 245.8 %reduce-scatter.14.cloned.1.call-start = ((), (), s32[]{:S(2)}) async-start(), calls=%async_computation.16 | async-start | bytes 11796480 | tf_op jit(solution)/shard_map/reduce_scatter | solution.py:225
  280.9 40.2 %copy-start.26 = (f32[256]{0:T(256)S(1)}, f32[256]{0:T(256)}, u32[]{:S(2)}) copy-start(f32[256]{0:T(256)} %copy-done.25) | copy-start | bytes 3076
  281.0 40.2 %copy-start.28 = (f32[256]{0:T(256)S(1)}, f32[256]{0:T(256)}, u32[]{:S(2)}) copy-start(f32[256]{0:T(256)} %copy-done.27) | copy-start | bytes 3076
  281.0 302.9 %reduce-scatter.8.cloned.1.call-start = ((), (), s32[]{:S(2)}) async-start(), calls=%async_computation.13 | async-start | bytes 8847360 | tf_op jit(solution)/shard_map/reduce_scatter | solution.py:217
  326.3 499.0 %all-reduce.20.cloned.1.call-start = ((), (), s32[]{:S(2)}) async-start(), calls=%async_computation.17 | async-start | bytes 14155776 | tf_op jit(solution)/shard_map/psum | solution.py:228
  (37 other events, 187.0 us)
Sparse Core Ops, SparseCore 0:
  9.6 33.6 all-gather.9
  44.8 37.5 all-gather.19
  84.6 19.6 all-gather.11
  106.3 19.6 all-gather.13
  127.4 17.4 all-gather.15
  146.3 37.4 all-gather.17
  185.9 28.5 all-gather.21
  261.2 58.3 reduce-scatter.5
  322.9 33.0 reduce-scatter.9
  358.5 78.3 reduce-scatter.11
  439.4 78.3 reduce-scatter.13
  520.2 63.6 reduce-scatter.7
  588.9 236.3 all-reduce.19
where the time goes:
time: 844 us; the launch traced here: 839 us
  waiting for transfers between devices  580 us (69%)
  matrix products  113 us (13%)
  blocking collectives  74.8 us (9%)
  local copies, waits for them, and re-layouts  30.1 us (4%)
  other arithmetic  22.6 us (3%)
  between operations  17.2 us (2%)
    psum x1, waiting for transfers between devices, body(): lax.psum((owned[0], owned[1], owned[2], owned[3], owned[4], owned[5], own...  178 us
    reduce_scatter x1, waiting for transfers between devices, body(): lax.psum_scatter(grad_down, 'cp', scatter_dimension=0, tiled=True)  81 us
    reduce_scatter x1, waiting for transfers between devices, body(): lax.psum_scatter(grad_in, 'cp', scatter_dimension=0, tiled=True)  80.8 us
    reduce_scatter x1, waiting for transfers between devices, body(): lax.psum_scatter(grad_qkv, 'cp', scatter_dimension=0, tiled=True)  66.1 us
    psum x1, blocking collectives, body(): lax.psum((owned[0], owned[1], owned[2], owned[3], owned[4], owned[5], own...  39.2 us
    all_gather x1, waiting for transfers between devices, body(): lax.all_gather(w_in, 'cp', axis=0, tiled=True)  36.8 us
    reduce_scatter x1, waiting for transfers between devices, body(): lax.psum_scatter(grad_out_proj, 'cp', scatter_dimension=0, tiled=True)  29.6 us
    reduce_scatter x1, waiting for transfers between devices, body(): owned_terms = lax.psum_scatter(terms, 'cp', scatter_dimension=0, tiled=True)  25.7 us
  transfers between devices with their start and end apart: 13, of which 13 were waited for; matrix products, arithmetic and copies ran while one was open for 13% of the time, Pallas kernels for 0%

commit v1 on v0

--- a/solution.py
+++ b/solution.py
@@ -3,6 +3,8 @@
 import jax
 import jax.numpy as jnp
 from jax import lax
+from jax.experimental import pallas as pl
+from jax.experimental.pallas import tpu as pltpu
 from jax.sharding import PartitionSpec as P
 
 D = 768
@@ -245,6 +247,499 @@
     return (layer_out, input_grad) + tuple(totals)
 
 
+BF = jnp.bfloat16
+F32 = jnp.float32
+MESH = pl.DeviceIdType.MESH
+VM = pl.BlockSpec(memory_space=pltpu.VMEM)
+CHUNKS = 4
+
+
+def params(collective_id=None, **more):
+    if collective_id is not None:
+        more.update(collective_id=collective_id, has_side_effects=True)
+    return pltpu.CompilerParams(vmem_limit_bytes=48 * 2**20, **more)
+
+
+def places():
+    me = lax.axis_index("cp")
+    core = lax.rem(me, 2)
+    row = me // 2
+    return me, row * 2 + 1 - core, (1 - row) * 2 + core, (1 - row) * 2 + 1 - core
+
+
+def greet(*others):
+    barrier = pltpu.get_barrier_semaphore()
+    for other in others:
+        pl.semaphore_signal(barrier, inc=1, device_id={"cp": other}, device_id_type=MESH)
+    pl.semaphore_wait(barrier, len(others))
+
+
+def push(src, dst, send, recv, other):
+    return pltpu.make_async_remote_copy(
+        src_ref=src, dst_ref=dst, send_sem=send, recv_sem=recv,
+        device_id={"cp": other}, device_id_type=MESH,
+    )
+
+
+def open_kernel(x_ref, w_ref, s_ref, xa_ref, wa_ref, sa_ref, send, recv):
+    me, sib, opp, diag = places()
+    greet(sib, opp, diag)
+    part = x_ref.shape[0] // CHUNKS
+    pieces = [pl.ds(k * part, part) for k in range(CHUNKS)]
+    across = [
+        push(x_ref.at[p], xa_ref.at[me, p], send.at[k], recv.at[k], opp)
+        for k, p in enumerate(pieces)
+    ]
+    slot = CHUNKS
+    rest = []
+    for other in (opp, diag, sib):
+        rest.append(push(s_ref, sa_ref.at[me], send.at[slot], recv.at[slot], other))
+        rest.append(push(w_ref.at[other], wa_ref.at[me], send.at[slot + 1], recv.at[slot + 1], other))
+        slot += 2
+    rest.append(push(x_ref, xa_ref.at[me], send.at[slot], recv.at[slot], sib))
+    slot += 1
+    for copy in across + rest:
+        copy.start()
+    xa_ref[me] = x_ref[...]
+    wa_ref[me] = w_ref[me]
+    sa_ref[me] = s_ref[...]
+    onward = []
+    for k, p in enumerate(pieces):
+        across[k].wait_recv()
+        copy = push(xa_ref.at[opp, p], xa_ref.at[opp, p], send.at[slot + k], recv.at[slot + k], sib)
+        copy.start()
+        onward.append(copy)
+    for copy in across:
+        copy.wait_send()
+    for copy in rest + onward:
+        copy.wait()
+
+
+def open_exchange(x, w, s):
+    n = w.shape[0]
+    count = 2 * CHUNKS + 7
+    return pl.pallas_call(
+        open_kernel,
+        out_shape=[
+            jax.ShapeDtypeStruct((n,) + x.shape, x.dtype),
+            jax.ShapeDtypeStruct(w.shape, w.dtype),
+            jax.ShapeDtypeStruct((n,) + s.shape, s.dtype),
+        ],
+        in_specs=[VM] * 3,
+        out_specs=[VM] * 3,
+        scratch_shapes=[pltpu.SemaphoreType.DMA((count,))] * 2,
+        compiler_params=params(0),
+        name="open_exchange",
+    )(x, w, s)
+
+
+def swap_kernel(w_ref, wa_ref, send, recv):
+    me, sib, opp, diag = places()
+    greet(sib, opp, diag)
+    copies = []
+    for k, other in enumerate((opp, diag, sib)):
+        copies.append(push(w_ref.at[other], wa_ref.at[me], send.at[k], recv.at[k], other))
+        copies[-1].start()
+    wa_ref[me] = w_ref[me]
+    for copy in copies:
+        copy.wait()
+
+
+def swap(w, collective_id):
+    return pl.pallas_call(
+        swap_kernel,
+        out_shape=jax.ShapeDtypeStruct(w.shape, w.dtype),
+        in_specs=[VM],
+        out_specs=VM,
+        scratch_shapes=[pltpu.SemaphoreType.DMA((3,))] * 2,
+        compiler_params=params(collective_id),
+        name="swap",
+    )(w)
+
+
+class Reduce:
+    def __init__(self, p_ref, near, sent, far, send, recv):
+        self.me, self.sib, self.opp, self.diag = places()
+        self.refs = (p_ref, near, sent, far)
+        self.part = part = p_ref.shape[1] // CHUNKS
+        self.pieces = [pl.ds(k * part, part) for k in range(CHUNKS)]
+        self.first, self.own, self.across = [], [], []
+        for k, p in enumerate(self.pieces):
+            self.first.append(push(p_ref.at[self.diag, p], near.at[0, p], send.at[k], recv.at[k], self.sib))
+            self.own.append(push(p_ref.at[self.sib, p], near.at[1, p], send.at[CHUNKS + k], recv.at[CHUNKS + k], self.sib))
+            self.across.append(push(sent.at[p], far.at[p], send.at[2 * CHUNKS + k], recv.at[2 * CHUNKS + k], self.opp))
+
+    def start(self):
+        p_ref, near, sent, far = self.refs
+        for copy in self.first + self.own:
+            copy.start()
+        for k, p in enumerate(self.pieces):
+            self.first[k].wait_recv()
+            sent[p] = (p_ref[self.opp, p].astype(F32) + near[0, p].astype(F32)).astype(BF)
+            self.across[k].start()
+
+    def piece(self, k):
+        p_ref, near, sent, far = self.refs
+        p = self.pieces[k]
+        self.own[k].wait_recv()
+        self.across[k].wait_recv()
+        return p_ref[self.me, p].astype(F32) + near[1, p].astype(F32) + far[p].astype(F32)
+
+    def finish(self):
+        for copy in self.first + self.own + self.across:
+            copy.wait_send()
+
+
+class Gather:
+    def __init__(self, x_ref, all_ref, send, recv, base):
+        self.me, self.sib, self.opp, self.diag = places()
+        part = x_ref.shape[0] // CHUNKS
+        self.pieces = [pl.ds(k * part, part) for k in range(CHUNKS)]
+        self.across, self.near, self.onward = [], [], []
+        me, sib, opp = self.me, self.sib, self.opp
+        for k, p in enumerate(self.pieces):
+            a, b, c = base + k, base + CHUNKS + k, base + 2 * CHUNKS + k
+            self.across.append(push(x_ref.at[p], all_ref.at[me, p], send.at[a], recv.at[a], opp))
+            self.near.append(push(x_ref.at[p], all_ref.at[me, p], send.at[b], recv.at[b], sib))
+            self.onward.append(push(all_ref.at[opp, p], all_ref.at[opp, p], send.at[c], recv.at[c], sib))
+
+    def start(self, k):
+        self.across[k].start()
+        self.near[k].start()
+
+    def finish(self):
+        for k in range(CHUNKS):
+            self.across[k].wait_recv()
+            self.onward[k].start()
+        for copy in self.across:
+            copy.wait_send()
+        for copy in self.near + self.onward:
+            copy.wait()
+
+
+def normalise(values):
+    centred = values - jnp.mean(values, axis=-1, keepdims=True)
+    variance = jnp.mean(centred * centred, axis=-1, keepdims=True)
+    scale = lax.rsqrt(variance + 1e-05)
+    return centred * scale, scale
+
+
+def norm_back(upstream, gain, unit, scale):
+    inner = upstream * gain
+    return scale * (
+        inner
+        - jnp.mean(inner, axis=-1, keepdims=True)
+        - unit * jnp.mean(inner * unit, axis=-1, keepdims=True)
+    )
+
+
+def middle_kernel(p_ref, x_ref, vec_ref, r_ref, all_ref, near, sent, far, mine, send, recv):
+    me, sib, opp, diag = places()
+    greet(sib, opp)
+    reduce = Reduce(p_ref, near, sent, far, send, recv)
+    gather = Gather(mine, all_ref, send, recv, 3 * CHUNKS)
+    reduce.start()
+    for k, p in enumerate(reduce.pieces):
+        r = x_ref[p].astype(F32) + (reduce.piece(k) + vec_ref[0:1])
+        r_ref[p] = r
+        unit, _ = normalise(r)
+        low = (unit * vec_ref[1:2] + vec_ref[2:3]).astype(BF)
+        mine[p] = low
+        gather.start(k)
+        all_ref[me, p] = low
+    gather.finish()
+    reduce.finish()
+
+
+def reduce_scratch(rows, wide):
+    return [
+        pltpu.VMEM((2, rows, wide), BF),
+        pltpu.VMEM((rows, wide), BF),
+        pltpu.VMEM((rows, wide), BF),
+    ]
+
+
+def middle_step(p, x, vec):
+    n, rows, wide = p.shape
+    return pl.pallas_call(
+        middle_kernel,
+        out_shape=[
+            jax.ShapeDtypeStruct((rows, wide), F32),
+            jax.ShapeDtypeStruct((n, rows, wide), BF),
+        ],
+        in_specs=[VM] * 3,
+        out_specs=[VM] * 2,
+        scratch_shapes=reduce_scratch(rows, wide)
+        + [pltpu.VMEM((rows, wide), BF)]
+        + [pltpu.SemaphoreType.DMA((6 * CHUNKS,))] * 2,
+        compiler_params=params(1),
+        name="middle_step",
+    )(p, x, vec)
+
+
+def back_kernel(p_ref, r_ref, g_ref, vec_ref, gr_ref, all_ref, sums_ref, near, sent, far, mine, send, recv):
+    me, sib, opp, diag = places()
+    greet(sib, opp)
+    reduce = Reduce(p_ref, near, sent, far, send, recv)
+    gather = Gather(mine, all_ref, send, recv, 3 * CHUNKS)
+    reduce.start()
+    sums_ref[...] = jnp.zeros_like(sums_ref)
+    for k, p in enumerate(reduce.pieces):
+        unit, scale = normalise(r_ref[p])
+        g = g_ref[p].astype(F32)
+        upstream = reduce.piece(k)
+        gr = g + norm_back(upstream, vec_ref[1:2], unit, scale)
+        gr_ref[p] = gr
+        low = gr.astype(BF)
+        mine[p] = low
+        gather.start(k)
+        all_ref[me, p] = low
+        sums_ref[0:1] += jnp.sum(upstream * unit, axis=0, keepdims=True)
+        sums_ref[1:2] += jnp.sum(upstream, axis=0, keepdims=True)
+        sums_ref[2:3] += jnp.sum(low.astype(F32), axis=0, keepdims=True)
+        sums_ref[3:4] += jnp.sum(g, axis=0, keepdims=True)
+    gather.finish()
+    reduce.finish()
+
+
+def back_step(p, r, g, vec):
+    n, rows, wide = p.shape
+    return pl.pallas_call(
+        back_kernel,
+        out_shape=[
+            jax.ShapeDtypeStruct((rows, wide), F32),
+            jax.ShapeDtypeStruct((n, rows, wide), BF),
+            jax.ShapeDtypeStruct((8, wide), F32),
+        ],
+        in_specs=[VM] * 4,
+        out_specs=[VM] * 3,
+        scratch_shapes=reduce_scratch(rows, wide)
+        + [pltpu.VMEM((rows, wide), BF)]
+        + [pltpu.SemaphoreType.DMA((6 * CHUNKS,))] * 2,
+        compiler_params=params(2),
+        name="back_step",
+    )(p, r, g, vec)
+
+
+def last_kernel(p_ref, x_ref, gr_ref, vec_ref, out_ref, sums_ref, near, sent, far, send, recv):
+    me, sib, opp, diag = places()
+    greet(sib, opp)
+    reduce = Reduce(p_ref, near, sent, far, send, recv)
+    reduce.start()
+    sums_ref[...] = jnp.zeros_like(sums_ref)
+    for k, p in enumerate(reduce.pieces):
+        unit, scale = normalise(x_ref[p].astype(F32))
+        upstream = reduce.piece(k)
+        out_ref[p] = (gr_ref[p] + norm_back(upstream, vec_ref[0:1], unit, scale)).astype(BF)
+        sums_ref[0:1] += jnp.sum(upstream * unit, axis=0, keepdims=True)
+        sums_ref[1:2] += jnp.sum(upstream, axis=0, keepdims=True)
+    reduce.finish()
+
+
+def last_step(p, x, gr, vec):
+    n, rows, wide = p.shape
+    return pl.pallas_call(
+        last_kernel,
+        out_shape=[
+            jax.ShapeDtypeStruct((rows, wide), BF),
+            jax.ShapeDtypeStruct((8, wide), F32),
+        ],
+        in_specs=[VM] * 4,
+        out_specs=[VM] * 2,
+        scratch_shapes=reduce_scratch(rows, wide)
+        + [pltpu.SemaphoreType.DMA((3 * CHUNKS,))] * 2,
+        compiler_params=params(3),
+        name="last_step",
+    )(p, x, gr, vec)
+
+
+def head_mask(wide):
+    lane = lax.broadcasted_iota(jnp.int32, (1, wide), 1)
+    low = pl.program_id(0) * HD
+    return (lane >= low) & (lane < low + HD)
+
+
+def causal(block, first, count):
+    row = lax.broadcasted_iota(jnp.int32, (block, count), 0) + first
+    return row >= lax.broadcasted_iota(jnp.int32, (block, count), 1)
+
+
+def attend_kernel(block, q_ref, k_ref, v_ref, o_ref, lse_ref):
+    length, wide = q_ref.shape
+    mask = head_mask(wide)
+    for first in range(0, length, block):
+        count = first + block
+        rows = slice(first, count)
+        q = jnp.where(mask, q_ref[rows], 0) * BF(HD**-0.5)
+        s = jnp.where(causal(block, first, count), along_rows(q, k_ref[:count]), -1e30)
+        top = jnp.max(s, axis=-1, keepdims=True)
+        p = jnp.exp(s - top)
+        total = jnp.sum(p, axis=-1, keepdims=True)
+        o = jnp.dot(p.astype(BF), v_ref[:count], preferred_element_type=F32) / total
+        o_ref[rows] = jnp.where(mask, o.astype(BF), o_ref[rows])
+        lse_ref[0, rows] = jnp.broadcast_to(top + jnp.log(total), (block, 128))
+
+
+def attend(q, k, v):
+    length, wide = q.shape
+    heads = wide // HD
+    whole = pl.BlockSpec((length, wide), lambda h: (0, 0))
+    return pl.pallas_call(
+        partial(attend_kernel, min(256, length)),
+        grid=(heads,),
+        out_shape=[
+            jax.ShapeDtypeStruct((length, wide), BF),
+            jax.ShapeDtypeStruct((heads, length, 128), F32),
+        ],
+        in_specs=[whole] * 3,
+        out_specs=[whole, pl.BlockSpec((1, length, 128), lambda h: (h, 0, 0))],
+        compiler_params=params(),
+        cost_estimate=pl.CostEstimate(flops=4 * heads * length * length * 256, bytes_accessed=8 * length * wide, transcendentals=heads * length * length),
+        name="attend",
+    )(q, k, v)
+
+
+def attend_back_kernel(block, q_ref, k_ref, v_ref, go_ref, lse_ref, gq_ref, gk_ref, gv_ref, gk_sum, gv_sum):
+    length, wide = q_ref.shape
+    mask = head_mask(wide)
+
+    @pl.when(pl.program_id(0) == 0)
+    def _():
+        gk_sum[...] = jnp.zeros_like(gk_sum)
+        gv_sum[...] = jnp.zeros_like(gv_sum)
+
+    for first in range(0, length, block):
+        count = first + block
+        rows = slice(first, count)
+        q = jnp.where(mask, q_ref[rows], 0) * BF(HD**-0.5)
+        go = jnp.where(mask, go_ref[rows], 0)
+        s = along_rows(q, k_ref[:count])
+        p = jnp.where(causal(block, first, count), jnp.exp(s - lse_ref[0, rows, 0:1]), 0.0)
+        dp = along_rows(go, v_ref[:count])
+        delta = jnp.sum(p * dp, axis=-1, keepdims=True)
+        ds = (p * (dp - delta)).astype(BF)
+        gq = jnp.dot(ds, k_ref[:count], preferred_element_type=F32) * HD**-0.5
+        gq_ref[rows] = jnp.where(mask, gq.astype(BF), gq_ref[rows])
+        gk_sum[:count] += across_rows(ds, q)
+        gv_sum[:count] += across_rows(p.astype(BF), go)
+
+    @pl.when(pl.program_id(0) == pl.num_programs(0) - 1)
+    def _():
+        gk_ref[...] = gk_sum[...].astype(BF)
+        gv_ref[...] = gv_sum[...].astype(BF)
+
+
+def attend_back(q, k, v, go, lse):
+    length, wide = q.shape
+    heads = wide // HD
+    whole = pl.BlockSpec((length, wide), lambda h: (0, 0))
+    return pl.pallas_call(
+        partial(attend_back_kernel, min(256, length)),
+        grid=(heads,),
+        out_shape=[jax.ShapeDtypeStruct((length, wide), BF)] * 3,
+        in_specs=[whole] * 4 + [pl.BlockSpec((1, length, 128), lambda h: (h, 0, 0))],
+        out_specs=[whole] * 3,
+        scratch_shapes=[pltpu.VMEM((length, wide), F32)] * 2,
+        compiler_params=params(),
+        cost_estimate=pl.CostEstimate(flops=10 * heads * length * length * 256, bytes_accessed=16 * length * wide, transcendentals=heads * length * length),
+        name="attend_back",
+    )(q, k, v, go, lse)
+
+
+def turn(blocks, n):
+    me = lax.axis_index("cp")
+    result = jnp.zeros_like(blocks)
+    result = lax.dynamic_update_index_in_dim(result, lax.dynamic_index_in_dim(blocks, me, 0), me, 0)
+    for step in range(1, n):
+        there, back = lax.rem(me + step, n), lax.rem(me + n - step, n)
+        got = lax.ppermute(
+            lax.dynamic_index_in_dim(blocks, there, 0), "cp", [(i, (i + step) % n) for i in range(n)]
+        )
+        result = lax.dynamic_update_index_in_dim(result, got, back, 0)
+    return result
+
+
+def head_body(
+    tokens, cotangent, ln1_gain, ln1_bias, w_qkv, b_qv, w_out, b_out,
+    ln2_gain, ln2_bias, w_in, b_in, w_down, b_down, *, n,
+):
+    rows = tokens.shape[0]
+    length = rows * n
+    me = lax.axis_index("cp")
+    share = D // n
+    ff_share = w_in.shape[1] // n
+    tidy = jnp.concatenate([ln1_gain, ln1_bias, b_out, ln2_gain, ln2_bias, b_down, b_qv])
+    tidy = jnp.concatenate([tidy, jnp.zeros((-tidy.shape[0] % 2048,), BF)]).reshape(-1, 128)
+    w_blocks = w_qkv.reshape(share, 3, n, share).transpose(2, 0, 1, 3).reshape(n, share, 3 * share)
+    in_cols = turn(w_in.reshape(share, n, ff_share).transpose(1, 0, 2), n).reshape(D, ff_share)
+    cot_all = lax.all_gather(cotangent, "cp", axis=0, tiled=True)
+    x_all, w_mine, tidy_all = open_exchange(tokens, w_blocks, tidy)
+    w_mine = w_mine.reshape(D, 3 * share)
+    tidy_all = tidy_all.reshape(n, -1).astype(F32)
+    gain_one, shift_one, out_bias, gain_two, shift_two, down_bias = (
+        tidy_all[:, i * share : (i + 1) * share].reshape(D) for i in range(6)
+    )
+    qv_bias = tidy_all[:, 6 * share : 8 * share].reshape(2, D)
+    qv_mine = lax.dynamic_slice_in_dim(qv_bias, me * share, share, 1)
+    vec_two = jnp.concatenate([jnp.stack([out_bias, gain_two, shift_two]), jnp.zeros((5, D), F32)])
+    vec_one = jnp.concatenate([gain_one[None], jnp.zeros((7, D), F32)])
+
+    n1 = layer_norm(x_all.reshape(length, D).astype(F32), gain_one, shift_one).astype(BF)
+    mixed = jnp.dot(n1, w_mine, preferred_element_type=F32)
+    q = (mixed[:, :share] + qv_mine[0]).astype(BF)
+    k = mixed[:, share : 2 * share].astype(BF)
+    v = (mixed[:, 2 * share :] + qv_mine[1]).astype(BF)
+    o, lse = attend(q, k, v)
+    o_part = jnp.dot(o, w_out, preferred_element_type=F32).astype(BF).reshape(n, rows, D)
+    r, n2 = middle_step(o_part, tokens, vec_two)
+    n2 = n2.reshape(length, D)
+    hidden = jnp.dot(n2, in_cols, preferred_element_type=F32) + b_in.astype(F32)
+    active, gelu_back = jax.vjp(partial(jax.nn.gelu, approximate=True), hidden)
+    a = active.astype(BF)
+    y_part = jnp.dot(a, w_down, preferred_element_type=F32).astype(BF)
+    y = lax.psum_scatter(y_part, "cp", scatter_dimension=0, tiled=True)
+    layer_out = (r + y.astype(F32) + down_bias).astype(BF)
+
+    gu = gelu_back(along_rows(cot_all, w_down))[0].astype(BF)
+    n2_part = along_rows(gu, in_cols).astype(BF).reshape(n, rows, D)
+    grad_down = across_rows(a, cot_all).astype(BF)
+    grad_in = turn(across_rows(n2, gu).astype(BF).reshape(n, share, ff_share), n)
+    grad_in = grad_in.transpose(1, 0, 2).reshape(share, n * ff_share)
+    grad_in_bias = jnp.sum(gu.astype(F32), axis=0)
+    grad_down = lax.psum(grad_down, "rep").astype(F32)
+    grad_in = lax.psum(grad_in, "rep").astype(F32)
+
+    gr, gz, sums_two = back_step(n2_part, r, cotangent, vec_two)
+    gz = gz.reshape(length, D)
+    go = along_rows(gz, w_out).astype(BF)
+    grad_out = lax.psum(across_rows(o, gz).astype(BF), "rep").astype(F32)
+    gq, gk, gv = attend_back(q, k, v, go, lse)
+    gm = jnp.concatenate([gq, gk, gv], axis=1)
+    grad_qkv = swap(across_rows(n1, gm).astype(BF).reshape(n, share, 3 * share), 4)
+    grad_qkv = grad_qkv.reshape(n, share, 3, share).transpose(1, 2, 0, 3).reshape(share, 3 * D)
+    grad_qkv = lax.psum(grad_qkv, "rep").astype(F32)
+    n1_part = along_rows(gm, w_mine).astype(BF).reshape(n, rows, D)
+    input_grad, sums_one = last_step(n1_part, tokens, gr, vec_one)
+
+    qv_sums = jnp.zeros((2, D), F32)
+    qv_sums = lax.dynamic_update_slice(
+        qv_sums,
+        jnp.stack([jnp.sum(gq.astype(F32), axis=0), jnp.sum(gv.astype(F32), axis=0)]),
+        (0, me * share),
+    )
+    in_sums = lax.dynamic_update_slice(jnp.zeros((n * ff_share,), F32), grad_in_bias, (me * ff_share,))
+    sums = lax.psum(
+        jnp.concatenate([sums_one[:2], sums_two[:4], qv_sums, in_sums.reshape(-1, D)]), ("rep", "cp")
+    )
+    own = lax.dynamic_slice_in_dim(sums[:6], me * share, share, 1)
+    own_qv = lax.dynamic_slice_in_dim(sums[6:8].reshape(-1), me * 2 * share, 2 * share, 0)
+    own_in = lax.dynamic_slice_in_dim(sums[8:].reshape(-1), me * ff_share, ff_share, 0)
+    return (
+        layer_out, input_grad, own[0], own[1], grad_qkv, own_qv, grad_out, own[4],
+        own[2], own[3], grad_in, own_in, grad_down, own[5],
+    )
+
+
 def solution(mesh):
     placed = (
         P(("rep", "cp"), None),
@@ -262,8 +757,10 @@
         P("cp", None),
         P("cp"),
     )
+    count = mesh.shape["cp"]
+    by_heads = count == 4 and H % count == 0
     return jax.shard_map(
-        body,
+        partial(head_body, n=count) if by_heads else body,
         mesh=mesh,
         in_specs=placed,
         out_specs=(

time: 844 us -> 381 us (0.45)
  waiting for transfers between devices: 580 us -> 79.2 us
  Pallas kernels: 0 us -> 134 us
  matrix products: 113 us -> 27.8 us
  blocking collectives: 74.8 us -> 42.4 us
  local copies, waits for them, and re-layouts: 30.1 us -> 54.9 us
    reduce_scatter x5 -> x1, waiting for transfers between devices: 283 us -> 0.01 us  [head_body(): y = lax.psum_scatter(y_part, 'cp', scatter_dimension=0, tiled=True)]
    pallas_call x0 -> x7, Pallas kernels: none -> 134 us  [the longest x1 39.2 us: back_step(): pl.pallas_call(back_kernel, out_shape=[jax.ShapeDtypeStruct((rows, wide),...]
    all_gather x7 -> x1, waiting for transfers between devices: 116 us -> 0.02 us  [head_body(): cot_all = lax.all_gather(cotangent, 'cp', axis=0, tiled=True)]
    psum x1, waiting for transfers between devices: 178 us -> 78.4 us  [head_body(): grad_qkv = lax.psum(grad_qkv, 'rep').astype(F32)]
    dot_general x10 -> x4, matrix products: 80.8 us -> 7.53 us  [the longest x1 3.24 us: head_body(): y_part = jnp.dot(a, w_down, preferred_element_type=F32).astype(BF)]
    unnamed x2 -> x0, blocking collectives: 25.1 us -> none
    reshape x0 -> x10, local copies, waits for them, and re-layouts: none -> 14.6 us  [the longest x3 6.11 us: head_body(): w_qkv.reshape(share, 3, n, share).transpose(2, 0, 1, 3)]
    dot_general x4, matrix products: 22.8 us -> 9.53 us  [across_rows(): lax.dot_general(left, right, (((0,), (0,)), ((), ())), preferred_element_...]
  transfers between devices with their start and end apart: 13 -> 9, of which waited for: 13 -> 1; matrix products, arithmetic and copies ran while one was open for 13% -> 22% of each run, Pallas kernels for 0% -> 36%
where the time goes in v1:
time: 381 us; the launch traced here: 376 us
  Pallas kernels  134 us (35%)
  waiting for transfers between devices  79.2 us (21%)
  local copies, waits for them, and re-layouts  54.9 us (14%)
  blocking collectives  42.4 us (11%)
  matrix products  27.8 us (7%)
  other arithmetic  16.1 us (4%)
  between operations  15.1 us (4%)
  starting transfers between devices  6.52 us (2%)
    psum x1, waiting for transfers between devices, head_body(): grad_qkv = lax.psum(grad_qkv, 'rep').astype(F32)  78.4 us
    psum x1, blocking collectives, head_body(): lax.psum(jnp.concatenate([sums_one[:2], sums_two[:4], qv_sums, in_sums.re...  42.4 us
    pallas_call x1, Pallas kernels, back_step(): pl.pallas_call(back_kernel, out_shape=[jax.ShapeDtypeStruct((rows, wide),...  39.2 us
    pallas_call x1, Pallas kernels, open_exchange(): pl.pallas_call(open_kernel, out_shape=[jax.ShapeDtypeStruct((n,) + x.shap...  30.6 us
    pallas_call x1, Pallas kernels, middle_step(): pl.pallas_call(middle_kernel, out_shape=[jax.ShapeDtypeStruct((rows, wide...  22.7 us
    unnamed x126, local copies, waits for them, and re-layouts  18.4 us
    pallas_call x1, Pallas kernels, swap(): pl.pallas_call(swap_kernel, out_shape=jax.ShapeDtypeStruct(w.shape, w.dty...  13.2 us
    pallas_call x1, Pallas kernels, last_step(): pl.pallas_call(last_kernel, out_shape=[jax.ShapeDtypeStruct((rows, wide),...  13.1 us
  transfers between devices with their start and end apart: 9, of which 1 were waited for; matrix products, arithmetic and copies ran while one was open for 22% of the time, Pallas kernels for 36%

profile of v1, /device:TPU:0, one launch (start us, length us, event | category | flops | bytes accessed | tf_op | source)
XLA Modules:
  0.0 375.7 jit_solution(3402917994151539383)
XLA Ops:
  8.0 2.7 reshape.162
  10.7 3.3 constant_dynamic-slice_fusion.5
  15.9 2.5 collective-permute-start.1
  20.7 2.1 reshape.155
  22.8 2.7 copy.65
  28.3 30.6 %open_exchange.1 = (bf16[4,256,768]{2,1,0:T(8,128)(2,1)S(1)}, bf16[4,192,576]{2,1,0:T(8,128)(2,1)S(1)}, bf16[4,16,128]{2,1,0:T(8,128)(2,1)S(1)}) custom-call(bf16[256,768]{1,0:T(8,128)(2,1)S(1)} %copy-done.4, bf16[4,192,576]{2,1,0:T(8,128)(2,1)S(1)} %copy-done.3, bf16[16,128]{1,0:T(8,128)(2,1)S(1)} %bitcast.88), custom_call_target="tpu_custom_call" | custom-call | tf_op jit(solution)/shard_map/open_exchange/pallas_call | solution.py:321
  68.5 2.4 copy.81
  70.9 2.4 copy.79
  76.0 5.1 %attend.1 = (bf16[1024,192]{1,0:T(8,128)(2,1)S(1)}, f32[3,1024,128]{2,1,0:T(8,128)S(1)}) custom-call(bf16[1024,192]{1,0:T(8,128)(2,1)S(1)} %get-tuple-element.79.q_ref, bf16[1024,192]{1,0:T(8,128)(2,1)S(1)} %copy-done.10, bf16[1024,192]{1,0:T(8,128)(2,1)S(1)} %get-tuple-element.78.v_ref), custom_call_target="tpu_custom_call" | custom-call | flops 3221225472 | bytes 1572864 | tf_op jit(solution)/shard_map/attend/pallas_call | solution.py:587
  86.6 22.7 %middle_step.1 = (f32[256,768]{1,0:T(8,128)S(1)}, bf16[4,256,768]{2,1,0:T(8,128)(2,1)S(1)}) custom-call(bf16[4,256,768]{2,1,0:T(8,128)(2,1)S(1)} %bitcast.84, bf16[256,768]{1,0:T(8,128)(2,1)S(1)} %copy-done.4, f32[8,768]{1,0:T(8,128)S(1)} %maximum_maximum_fusion.vec_ref), custom_call_target="tpu_custom_call" | custom-call | tf_op jit(solution)/shard_map/middle_step/pallas_call | solution.py:464
  116.7 3.2 convolution_convert_fusion.2
  120.0 6.0 %convert_reduce_fusion = (f32[768]{0:T(1024)S(1)}, bf16[1024,768]{1,0:T(8,128)(2,1)S(1)}) fusion(f32[1024,768]{1,0:T(8,128)} %copy-done.57, f32[768]{0:T(1024)S(1)} %convert_element_type.103, bf16[1024,768]{1,0:T(8,128)(2,1)} %all-gather.2.cloned.1.call-done, bf16[768,768]{1,0:T(8,128)(2,1)S(1)} %copy-done), kind=kOutput, calls=%fused_computation.14 | convolution fusion | flops 1226046720 | bytes 7477248 | tf_op jit(solution)/shard_map/dot_general | solution.py:22
  131.9 39.2 %back_step.1 = (f32[256,768]{1,0:T(8,128)S(1)}, bf16[4,256,768]{2,1,0:T(8,128)(2,1)S(1)}, f32[8,768]{1,0:T(8,128)S(1)}) custom-call(bf16[4,256,768]{2,1,0:T(8,128)(2,1)S(1)} %bitcast.86, f32[256,768]{1,0:T(8,128)S(1)} %copy-done.6, bf16[256,768]{1,0:T(8,128)(2,1)S(1)} %copy-done.7, f32[8,768]{1,0:T(8,128)S(1)} %maximum_maximum_fusion.vec_ref), custom_call_target="tpu_custom_call" | custom-call | tf_op jit(solution)/shard_map/back_step/pallas_call | solution.py:507
  174.1 5.5 %convolution_convert_fusion.4 = bf16[768,768]{1,0:T(8,128)(2,1)} fusion(bf16[1024,768]{1,0:T(8,128)(2,1)} %all-gather.2.cloned.1.call-done, f32[1024,768]{1,0:T(8,128)} %copy-done.57, f32[768]{0:T(1024)S(1)} %convert_element_type.103), kind=kOutput, calls=%fused_computation.23 | convolution fusion | flops 1216413696 | bytes 5901312 | tf_op jit(solution)/shard_map/dot_general | solution.py:28
  179.7 9.7 %attend_back.1 = (bf16[1024,192]{1,0:T(8,128)(2,1)S(1)}, bf16[1024,192]{1,0:T(8,128)(2,1)S(1)}, bf16[1024,192]{1,0:T(8,128)(2,1)S(1)}) custom-call(bf16[1024,192]{1,0:T(8,128)(2,1)S(1)} %copy-done.19, bf16[1024,192]{1,0:T(8,128)(2,1)S(1)} %copy-done.11, bf16[1024,192]{1,0:T(8,128)(2,1)S(1)} %copy-done.17, bf16[1024,192]{1,0:T(8,128)(2,1)S(1)} %copy.74.go_ref, ...), custom_call_target="tpu_custom_call" | custom-call | flops 8053063680 | bytes 3145728 | tf_op jit(solution)/shard_map/attend_back/pallas_call | solution.py:636
  193.4 13.2 %swap.1 = bf16[4,192,576]{2,1,0:T(8,128)(2,1)S(1)} custom-call(bf16[4,192,576]{2,1,0:T(8,128)(2,1)S(1)} %bitcast.85), custom_call_target="tpu_custom_call" | custom-call | tf_op jit(solution)/shard_map/swap/pallas_call | solution.py:349
  208.0 3.4 copy.77
  211.4 3.3 reshape.170
  219.2 2.7 convolution_convert_fusion
  222.0 13.1 %last_step.1 = (bf16[256,768]{1,0:T(8,128)(2,1)S(1)}, f32[8,768]{1,0:T(8,128)S(1)}) custom-call(bf16[4,256,768]{2,1,0:T(8,128)(2,1)S(1)} %bitcast.87, bf16[256,768]{1,0:T(8,128)(2,1)S(1)} %copy-done.4, f32[256,768]{1,0:T(8,128)S(1)} %copy-done.9, f32[8,768]{1,0:T(8,128)S(1)} %concatenate.18.vec_ref), custom_call_target="tpu_custom_call" | custom-call | tf_op jit(solution)/shard_map/last_step/pallas_call | solution.py:541
  235.6 42.4 %psum.35 = f32[12,768]{1,0:T(8,128)S(1)} all-reduce(f32[12,768]{1,0:T(8,128)S(1)} %pad_maximum_fusion.3), channel_id=1, replica_groups=mesh['rep'=8,'cp'=4] {'rep','cp'}, use_global_device_ids=true, to_apply=%region_6.7 | all-reduce | flops 9216 | bytes 73728 | tf_op jit(solution)/shard_map/psum | solution.py:731
  281.9 78.4 %all-reduce.4.cloned.1.call-done = (bf16[192,2304]{1,0:T(8,128)(2,1)}, bf16[192,768]{1,0:T(8,128)(2,1)}, bf16[192,3072]{1,0:T(8,128)(2,1)}, bf16[768,768]{1,0:T(8,128)(2,1)}) async-done(((bf16[192,2304]{1,0:T(8,128)(2,1)}, bf16[192,768]{1,0:T(8,128)(2,1)}, bf16[192,3072]{1,0:T(8,128)(2,1)}, bf16[768,768]{1,0:T(8,128)(2,1)}), (bf16[192,2304]{1,0:T(8,128)(2,1)}, bf16[192,768]{1,0:T(8,128)(2,1)}, ...) | async-done | bytes 3538960 | tf_op jit(solution)/shard_map/psum | solution.py:720
  360.4 1.9 convert_element_type.121
  362.3 2.5 convert_element_type.119
  (216 shorter events, 59.6 us)
Async XLA Ops:
  7.2 109.5 %copy-start = (bf16[768,768]{1,0:T(8,128)(2,1)S(1)}, bf16[768,768]{1,0:T(8,128)(2,1)}, u32[]{:S(2)}) copy-start(bf16[768,768]{1,0:T(8,128)(2,1)} %param.26) | copy-start | bytes 3538948
  7.2 112.8 %all-gather.2.cloned.1.call-start = ((), (), s32[]{:S(2)}) async-start(), calls=%async_computation.2 | async-start | bytes 1966080 | tf_op jit(solution)/shard_map/all_gather | solution.py:675
  7.9 272.2 %reduce-scatter.2.cloned.1.call-start = ((), (), s32[]{:S(2)}) async-start(), calls=%async_computation.1 | async-start | bytes 1966080 | tf_op jit(solution)/shard_map/reduce_scatter | solution.py:700
  14.0 6.7 %copy-start.42 = (bf16[192,2304]{1,0:T(8,128)(2,1)S(1)}, bf16[192,2304]{1,0:T(8,128)(2,1)}, u32[]{:S(2)}) copy-start(bf16[192,2304]{1,0:T(8,128)(2,1)} %param.18) | copy-start | bytes 2654212
  14.7 94.6 %collective-permute-start = (bf16[1,192,768]{2,1,0:T(8,128)(2,1)}, bf16[1,192,768]{2,1,0:T(8,128)(2,1)}, u32[]{:S(2)}, u32[]{:S(2)}) collective-permute-start(bf16[1,192,768]{2,1,0:T(8,128)(2,1)} %bitcast.82), channel_id=1, source_target_pairs={{0,1},{1,2},{2,3},{3,0},{4,5},{5,6},{6,7},{7,4},{8,9},{9,10},{10,1... | collective-permute-start | bytes 884744 | tf_op jit(solution)/shard_map/ppermute | solution.py:655
  15.9 94.6 %collective-permute-start.1 = (bf16[1,192,768]{2,1,0:T(8,128)(2,1)}, bf16[1,192,768]{2,1,0:T(8,128)(2,1)}, u32[]{:S(2)}, u32[]{:S(2)}) collective-permute-start(bf16[1,192,768]{2,1,0:T(8,128)(2,1)} %bitcast.81), channel_id=1, source_target_pairs={{0,2},{1,3},{2,0},{3,1},{4,6},{5,7},{6,4},{7,5},{8,10},{9,11},{10,... | collective-permute-start | bytes 884744 | tf_op jit(solution)/shard_map/ppermute | solution.py:655
  19.2 92.4 %collective-permute-start.2 = (bf16[1,192,768]{2,1,0:T(8,128)(2,1)}, bf16[1,192,768]{2,1,0:T(8,128)(2,1)}, u32[]{:S(2)}, u32[]{:S(2)}) collective-permute-start(bf16[1,192,768]{2,1,0:T(8,128)(2,1)} %bitcast.80), channel_id=1, source_target_pairs={{0,3},{1,0},{2,1},{3,2},{4,7},{5,4},{6,5},{7,6},{8,11},{9,8},{10,9... | collective-permute-start | bytes 884744 | tf_op jit(solution)/shard_map/ppermute | solution.py:655
  76.0 5.1 %copy-start.16 = (bf16[1024,192]{1,0:T(8,128)(2,1)}, bf16[1024,192]{1,0:T(8,128)(2,1)S(1)}, u32[]{:S(2)}) copy-start(bf16[1024,192]{1,0:T(8,128)(2,1)S(1)} %get-tuple-element.78.v_ref) | copy-start | bytes 1179652
  76.0 5.1 %copy-start.47 = (f32[1,2,4,128]{3,2,1,0:T(4,128)S(1)}, f32[1,2,4,128]{3,2,1,0:T(4,128)}, u32[]{:S(2)}) copy-start(f32[1,2,4,128]{3,2,1,0:T(4,128)} %get-tuple-element.74) | copy-start | bytes 12292
  76.0 5.1 %copy-start.48 = (f32[1,2,4,128]{3,2,1,0:T(4,128)S(1)}, f32[1,2,4,128]{3,2,1,0:T(4,128)}, u32[]{:S(2)}) copy-start(f32[1,2,4,128]{3,2,1,0:T(4,128)} %get-tuple-element.76) | copy-start | bytes 12292
  76.0 5.2 %copy-start.43 = (bf16[192,768]{1,0:T(8,128)(2,1)S(1)}, bf16[192,768]{1,0:T(8,128)(2,1)}, u32[]{:S(2)}) copy-start(bf16[192,768]{1,0:T(8,128)(2,1)} %param.20) | copy-start | bytes 884740
  86.2 23.1 %copy-start.39 = (bf16[4,192,768]{2,1,0:T(8,128)(2,1)S(1)}, bf16[4,192,768]{2,1,0:T(8,128)(2,1)}, u32[]{:S(2)}) copy-start(bf16[4,192,768]{2,1,0:T(8,128)(2,1)} %copy-done.38) | copy-start | bytes 3538948
  109.3 5.7 %copy-start.5 = (f32[256,768]{1,0:T(8,128)}, f32[256,768]{1,0:T(8,128)S(1)}, u32[]{:S(2)}) copy-start(f32[256,768]{1,0:T(8,128)S(1)} %get-tuple-element.33.r_ref) | copy-start | bytes 2359300
  109.3 5.7 %copy-start.22 = (bf16[4,256,768]{2,1,0:T(8,128)(2,1)}, bf16[4,256,768]{2,1,0:T(8,128)(2,1)S(1)}, u32[]{:S(2)}) copy-start(bf16[4,256,768]{2,1,0:T(8,128)(2,1)S(1)} %get-tuple-element.34) | copy-start | bytes 4718596
  119.9 6.0 %copy-start.23 = (bf16[4,256,768]{2,1,0:T(8,128)(2,1)S(1)}, bf16[4,256,768]{2,1,0:T(8,128)(2,1)}, u32[]{:S(2)}) copy-start(bf16[4,256,768]{2,1,0:T(8,128)(2,1)} %copy-done.22) | copy-start | bytes 4718596
  120.0 240.4 %all-reduce.4.cloned.1.call-start = ((), (), s32[]{:S(2)}) async-start(), calls=%async_computation.3 | async-start | bytes 7077888 | tf_op jit(solution)/shard_map/psum | solution.py:720
  128.5 87.2 %collective-permute-start.5 = (bf16[1,192,768]{2,1,0:T(8,128)(2,1)}, bf16[1,192,768]{2,1,0:T(8,128)(2,1)}, u32[]{:S(2)}, u32[]{:S(2)}) collective-permute-start(bf16[1,192,768]{2,1,0:T(8,128)(2,1)} %get-tuple-element.52), channel_id=1, source_target_pairs={{0,3},{1,0},{2,1},{3,2},{4,7},{5,4},{6,5},{7,6},{8,11},{9,8},{10,9... | collective-permute-start | bytes 884744 | tf_op jit(solution)/shard_map/ppermute | solution.py:655
  129.3 85.4 %collective-permute-start.4 = (bf16[1,192,768]{2,1,0:T(8,128)(2,1)}, bf16[1,192,768]{2,1,0:T(8,128)(2,1)}, u32[]{:S(2)}, u32[]{:S(2)}) collective-permute-start(bf16[1,192,768]{2,1,0:T(8,128)(2,1)} %get-tuple-element.53), channel_id=1, source_target_pairs={{0,2},{1,3},{2,0},{3,1},{4,6},{5,7},{6,4},{7,5},{8,10},{9,11},{10,... | collective-permute-start | bytes 884744 | tf_op jit(solution)/shard_map/ppermute | solution.py:655
  130.5 84.2 %collective-permute-start.3 = (bf16[1,192,768]{2,1,0:T(8,128)(2,1)}, bf16[1,192,768]{2,1,0:T(8,128)(2,1)S(1)}, u32[]{:S(2)}, u32[]{:S(2)}) collective-permute-start(bf16[1,192,768]{2,1,0:T(8,128)(2,1)} %get-tuple-element.54), channel_id=1, source_target_pairs={{0,1},{1,2},{2,3},{3,0},{4,5},{5,6},{6,7},{7,4},{8,9},{9,10},{10,1... | collective-permute-start | bytes 884744 | tf_op jit(solution)/shard_map/ppermute | solution.py:655
  174.1 5.5 %copy-start.11 = (bf16[1024,192]{1,0:T(8,128)(2,1)S(1)}, bf16[1024,192]{1,0:T(8,128)(2,1)}, u32[]{:S(2)}) copy-start(bf16[1024,192]{1,0:T(8,128)(2,1)} %copy.80.k_ref) | copy-start | bytes 1179652
  174.1 5.5 %copy-start.17 = (bf16[1024,192]{1,0:T(8,128)(2,1)S(1)}, bf16[1024,192]{1,0:T(8,128)(2,1)}, u32[]{:S(2)}) copy-start(bf16[1024,192]{1,0:T(8,128)(2,1)} %copy-done.16) | copy-start | bytes 1179652
  174.1 5.5 %copy-start.19 = (bf16[1024,192]{1,0:T(8,128)(2,1)S(1)}, bf16[1024,192]{1,0:T(8,128)(2,1)}, u32[]{:S(2)}) copy-start(bf16[1024,192]{1,0:T(8,128)(2,1)} %copy-done.18) | copy-start | bytes 1179652
  174.1 5.5 %copy-start.31 = (f32[3,1024,128]{2,1,0:T(8,128)S(1)}, f32[3,1024,128]{2,1,0:T(8,128)}, u32[]{:S(2)}) copy-start(f32[3,1024,128]{2,1,0:T(8,128)} %copy-done.30) | copy-start | bytes 4718596
  179.7 9.8 %copy-start.35 = (bf16[1024,768]{1,0:T(8,128)(2,1)S(1)}, bf16[1024,768]{1,0:T(8,128)(2,1)}, u32[]{:S(2)}) copy-start(bf16[1024,768]{1,0:T(8,128)(2,1)} %fusion.10) | copy-start | bytes 4718596
  (43 other events, 79.2 us)
Sparse Core Ops, SparseCore 0:
  9.6 30.8 all-gather.1
  120.1 37.6 reduce-scatter.1
  218.0 142.3 all-reduce.3

commit v2 on v1

--- a/solution.py
+++ b/solution.py
@@ -671,9 +671,10 @@
     tidy = jnp.concatenate([ln1_gain, ln1_bias, b_out, ln2_gain, ln2_bias, b_down, b_qv])
     tidy = jnp.concatenate([tidy, jnp.zeros((-tidy.shape[0] % 2048,), BF)]).reshape(-1, 128)
     w_blocks = w_qkv.reshape(share, 3, n, share).transpose(2, 0, 1, 3).reshape(n, share, 3 * share)
-    in_cols = turn(w_in.reshape(share, n, ff_share).transpose(1, 0, 2), n).reshape(D, ff_share)
-    cot_all = lax.all_gather(cotangent, "cp", axis=0, tiled=True)
     x_all, w_mine, tidy_all = open_exchange(tokens, w_blocks, tidy)
+    x_all, late_in, late_cot = lax.optimization_barrier((x_all, w_in, cotangent))
+    in_cols = turn(late_in.reshape(share, n, ff_share).transpose(1, 0, 2), n).reshape(D, ff_share)
+    cot_all = lax.all_gather(late_cot, "cp", axis=0, tiled=True)
     w_mine = w_mine.reshape(D, 3 * share)
     tidy_all = tidy_all.reshape(n, -1).astype(F32)
     gain_one, shift_one, out_bias, gain_two, shift_two, down_bias = (
@@ -697,27 +698,30 @@
     active, gelu_back = jax.vjp(partial(jax.nn.gelu, approximate=True), hidden)
     a = active.astype(BF)
     y_part = jnp.dot(a, w_down, preferred_element_type=F32).astype(BF)
-    y = lax.psum_scatter(y_part, "cp", scatter_dimension=0, tiled=True)
-    layer_out = (r + y.astype(F32) + down_bias).astype(BF)
-
     gu = gelu_back(along_rows(cot_all, w_down))[0].astype(BF)
     n2_part = along_rows(gu, in_cols).astype(BF).reshape(n, rows, D)
     grad_down = across_rows(a, cot_all).astype(BF)
-    grad_in = turn(across_rows(n2, gu).astype(BF).reshape(n, share, ff_share), n)
-    grad_in = grad_in.transpose(1, 0, 2).reshape(share, n * ff_share)
+    grad_in = across_rows(n2, gu).astype(BF).reshape(n, share, ff_share)
     grad_in_bias = jnp.sum(gu.astype(F32), axis=0)
-    grad_down = lax.psum(grad_down, "rep").astype(F32)
-    grad_in = lax.psum(grad_in, "rep").astype(F32)
+    grad_down = lax.psum(grad_down, "rep")
 
     gr, gz, sums_two = back_step(n2_part, r, cotangent, vec_two)
+    gz, y_part, grad_in = lax.optimization_barrier((gz, y_part, grad_in))
+    y = lax.psum_scatter(y_part, "cp", scatter_dimension=0, tiled=True)
+    layer_out = (r + y.astype(F32) + down_bias).astype(BF)
+    grad_in = turn(grad_in, n).transpose(1, 0, 2).reshape(share, n * ff_share)
     gz = gz.reshape(length, D)
     go = along_rows(gz, w_out).astype(BF)
-    grad_out = lax.psum(across_rows(o, gz).astype(BF), "rep").astype(F32)
+    grad_out = across_rows(o, gz).astype(BF)
+    grad_out, grad_in, grad_down = lax.optimization_barrier((grad_out, grad_in, grad_down))
+    grad_out, grad_in = lax.psum((grad_out, grad_in), "rep")
     gq, gk, gv = attend_back(q, k, v, go, lse)
     gm = jnp.concatenate([gq, gk, gv], axis=1)
     grad_qkv = swap(across_rows(n1, gm).astype(BF).reshape(n, share, 3 * share), 4)
     grad_qkv = grad_qkv.reshape(n, share, 3, share).transpose(1, 2, 0, 3).reshape(share, 3 * D)
+    grad_qkv, grad_out, grad_in = lax.optimization_barrier((grad_qkv, grad_out, grad_in))
     grad_qkv = lax.psum(grad_qkv, "rep").astype(F32)
+    grad_out, grad_in, grad_down = grad_out.astype(F32), grad_in.astype(F32), grad_down.astype(F32)
     n1_part = along_rows(gm, w_mine).astype(BF).reshape(n, rows, D)
     input_grad, sums_one = last_step(n1_part, tokens, gr, vec_one)
 

time: 381 us -> 422 us (1.11)
  waiting for transfers between devices: 79.2 us -> 127 us
  Pallas kernels: 134 us -> 108 us
  starting transfers between devices: 6.52 us -> 20.5 us
  local copies, waits for them, and re-layouts: 54.9 us -> 60.5 us
    psum x0 -> x2, waiting for transfers between devices: none -> 55.3 us  [the longest x1 36.1 us: head_body(): grad_out, grad_in = lax.psum((grad_out, grad_in), 'rep')]
    psum x1, waiting for transfers between devices: 78.4 us -> 59.7 us  [head_body(): grad_qkv = lax.psum(grad_qkv, 'rep').astype(F32)]
    pallas_call x1, Pallas kernels: 39.2 us -> 22.5 us  [back_step(): pl.pallas_call(back_kernel, out_shape=[jax.ShapeDtypeStruct((rows, wide),...]
    psum x0 -> x2, starting transfers between devices: none -> 13.9 us  [the longest x1 13.9 us: head_body(): grad_out, grad_in = lax.psum((grad_out, grad_in), 'rep')]
    ppermute x6, waiting for transfers between devices: 0.02 us -> 11.1 us  [turn(): lax.ppermute(lax.dynamic_index_in_dim(blocks, there, 0), 'cp', [(i, (i +...]
    pallas_call x1, Pallas kernels: 30.6 us -> 23.6 us  [open_exchange(): pl.pallas_call(open_kernel, out_shape=[jax.ShapeDtypeStruct((n,) + x.shap...]
    unnamed x126 -> x116, local copies, waits for them, and re-layouts: 18.4 us -> 24.3 us
  transfers between devices with their start and end apart: 9 -> 11, of which waited for: 1 -> 5; matrix products, arithmetic and copies ran while one was open for 22% -> 18% of each run, Pallas kernels for 36% -> 20%
where the time goes in v2:
time: 422 us; the launch traced here: 416 us
  waiting for transfers between devices  127 us (30%)
  Pallas kernels  108 us (26%)
  local copies, waits for them, and re-layouts  60.5 us (14%)
  blocking collectives  40.3 us (10%)
  matrix products  27.5 us (7%)
  starting transfers between devices  20.5 us (5%)
  other arithmetic  17.5 us (4%)
  between operations  14.8 us (4%)
    psum x1, waiting for transfers between devices, head_body(): grad_qkv = lax.psum(grad_qkv, 'rep').astype(F32)  59.7 us
    psum x1, blocking collectives, head_body(): lax.psum(jnp.concatenate([sums_one[:2], sums_two[:4], qv_sums, in_sums.re...  40.3 us
    psum x1, waiting for transfers between devices, head_body(): grad_out, grad_in = lax.psum((grad_out, grad_in), 'rep')  36.1 us
    unnamed x116, local copies, waits for them, and re-layouts  24.3 us
    pallas_call x1, Pallas kernels, open_exchange(): pl.pallas_call(open_kernel, out_shape=[jax.ShapeDtypeStruct((n,) + x.shap...  23.6 us
    pallas_call x1, Pallas kernels, back_step(): pl.pallas_call(back_kernel, out_shape=[jax.ShapeDtypeStruct((rows, wide),...  22.5 us
    pallas_call x1, Pallas kernels, middle_step(): pl.pallas_call(middle_kernel, out_shape=[jax.ShapeDtypeStruct((rows, wide...  21.5 us
    psum x1, waiting for transfers between devices, head_body(): grad_down = lax.psum(grad_down, 'rep')  19.2 us
  transfers between devices with their start and end apart: 11, of which 5 were waited for; matrix products, arithmetic and copies ran while one was open for 18% of the time, Pallas kernels for 20%

profile of v2, /device:TPU:0, one launch (start us, length us, event | category | flops | bytes accessed | tf_op | source)
XLA Modules:
  0.0 416.0 jit_solution(16889383338609773225)
XLA Ops:
  7.2 3.8 reshape.155
  11.0 2.5 copy.65
  16.3 23.6 %open_exchange.1 = (bf16[4,256,768]{2,1,0:T(8,128)(2,1)S(1)}, bf16[4,192,576]{2,1,0:T(8,128)(2,1)S(1)}, bf16[4,16,128]{2,1,0:T(8,128)(2,1)S(1)}) custom-call(bf16[256,768]{1,0:T(8,128)(2,1)S(1)} %copy-done.4, bf16[4,192,576]{2,1,0:T(8,128)(2,1)S(1)} %copy-done.3, bf16[16,128]{1,0:T(8,128)(2,1)S(1)} %bitcast.88), custom_call_target="tpu_custom_call" | custom-call | tf_op jit(solution)/shard_map/open_exchange/pallas_call | solution.py:321
  40.9 3.5 reshape.162
  44.4 5.9 %constant_dynamic-slice_fusion.5 = (bf16[192,1,768]{2,1,0:T(2,128)(2,1)S(1)}, bf16[192,1,768]{2,1,0:T(2,128)(2,1)S(1)}, bf16[192,1,768]{2,1,0:T(2,128)(2,1)S(1)}, bf16[192,1,768]{2,1,0:T(2,128)(2,1)}) fusion(bf16[192,4,768]{2,1,0:T(4,128)(2,1)} %reshape.162, s32[]{:T(128)S(6)} %select_n.41, s32[]{:T(128)S(6)} %select_n.42, s32[]{:T(128)S(6)} %select_n.40, ...), kind=kLoop, calls=%fused_computation.54 | loop fusion | bytes 2359312 | tf_op jit(solution)/shard_map/dynamic-slice.3
  67.8 2.7 add_convert_fusion.1
  75.9 5.0 %attend.1 = (bf16[1024,192]{1,0:T(8,128)(2,1)S(1)}, f32[3,1024,128]{2,1,0:T(8,128)S(1)}) custom-call(bf16[1024,192]{1,0:T(8,128)(2,1)S(1)} %copy-done.15, bf16[1024,192]{1,0:T(8,128)(2,1)S(1)} %copy-done.9, bf16[1024,192]{1,0:T(8,128)(2,1)S(1)} %copy-done.13), custom_call_target="tpu_custom_call" | custom-call | flops 3221225472 | bytes 1572864 | tf_op jit(solution)/shard_map/attend/pallas_call | solution.py:587
  85.7 21.5 %middle_step.1 = (f32[256,768]{1,0:T(8,128)S(1)}, bf16[4,256,768]{2,1,0:T(8,128)(2,1)S(1)}) custom-call(bf16[4,256,768]{2,1,0:T(8,128)(2,1)S(1)} %bitcast.84, bf16[256,768]{1,0:T(8,128)(2,1)S(1)} %copy-done.4, f32[8,768]{1,0:T(8,128)S(1)} %maximum_maximum_fusion.vec_ref), custom_call_target="tpu_custom_call" | custom-call | tf_op jit(solution)/shard_map/middle_step/pallas_call | solution.py:464
  114.6 3.2 convolution_convert_fusion.1
  117.9 5.3 %convolution_convert_fusion.4 = bf16[768,768]{1,0:T(8,128)(2,1)} fusion(bf16[1024,768]{1,0:T(8,128)(2,1)} %all-gather.2.cloned.1.call-done, f32[1024,768]{1,0:T(8,128)} %copy-done.52, f32[768]{0:T(1024)S(1)} %convert_element_type.103), kind=kOutput, calls=%fused_computation.23 | convolution fusion | flops 1216413696 | bytes 5901312 | tf_op jit(solution)/shard_map/dot_general | solution.py:28
  123.2 13.9 %all-reduce.10.cloned.1.call-start = ((), (), s32[]{:S(2)}) async-start(), calls=%async_computation.5 | async-start | bytes 2949120 | tf_op jit(solution)/shard_map/psum | solution.py:717
  137.1 5.7 %convert_reduce_fusion = (f32[768]{0:T(1024)S(1)}, bf16[1024,768]{1,0:T(8,128)(2,1)S(1)}) fusion(f32[1024,768]{1,0:T(8,128)} %copy-done.52, f32[768]{0:T(1024)S(1)} %convert_element_type.103, bf16[1024,768]{1,0:T(8,128)(2,1)} %all-gather.2.cloned.1.call-done, bf16[768,768]{1,0:T(8,128)(2,1)S(1)} %copy-done), kind=kOutput, calls=%fused_computation.14 | convolution fusion | flops 1226046720 | bytes 7477248 | tf_op jit(solution)/shard_map/dot_general | solution.py:22
  144.3 22.5 %back_step.1 = (f32[256,768]{1,0:T(8,128)S(1)}, bf16[4,256,768]{2,1,0:T(8,128)(2,1)S(1)}, f32[8,768]{1,0:T(8,128)S(1)}) custom-call(bf16[4,256,768]{2,1,0:T(8,128)(2,1)S(1)} %bitcast.86, f32[256,768]{1,0:T(8,128)S(1)} %copy-done.6, bf16[256,768]{1,0:T(8,128)(2,1)S(1)} %copy-done.8, f32[8,768]{1,0:T(8,128)S(1)} %maximum_maximum_fusion.vec_ref), custom_call_target="tpu_custom_call" | custom-call | tf_op jit(solution)/shard_map/back_step/pallas_call | solution.py:507
  173.1 2.8 collective-permute-done.3
  175.9 8.2 %collective-permute-done.4 = bf16[1,192,768]{2,1,0:T(8,128)(2,1)S(1)} collective-permute-done((bf16[1,192,768]{2,1,0:T(8,128)(2,1)S(1)}, bf16[1,192,768]{2,1,0:T(8,128)(2,1)S(1)}, u32[]{:S(2)}, u32[]{:S(2)}) %collective-permute-start.4) | collective-permute-done | bytes 294944 | tf_op jit(solution)/shard_map/ppermute | solution.py:655
  185.4 19.2 %all-reduce.6.cloned.1.call-done = bf16[768,768]{1,0:T(8,128)(2,1)} async-done(((bf16[768,768]{1,0:T(8,128)(2,1)}), bf16[768,768]{1,0:T(8,128)(2,1)}) %all-reduce.6.cloned.1.call-update) | async-done | bytes 1179664 | tf_op jit(solution)/shard_map/psum | solution.py:706
  214.8 9.5 %attend_back.1 = (bf16[1024,192]{1,0:T(8,128)(2,1)S(1)}, bf16[1024,192]{1,0:T(8,128)(2,1)S(1)}, bf16[1024,192]{1,0:T(8,128)(2,1)S(1)}) custom-call(bf16[1024,192]{1,0:T(8,128)(2,1)S(1)} %copy-done.16, bf16[1024,192]{1,0:T(8,128)(2,1)S(1)} %copy-done.10, bf16[1024,192]{1,0:T(8,128)(2,1)S(1)} %copy-done.14, bf16[1024,192]{1,0:T(8,128)(2,1)S(1)} %copy.74.go_ref, ...), custom_call_target="tpu_custom_call" | custom-call | flops 8053063680 | bytes 3145728 | tf_op jit(solution)/shard_map/attend_back/pallas_call | solution.py:636
  225.7 12.9 %last_step.1 = (bf16[256,768]{1,0:T(8,128)(2,1)S(1)}, f32[8,768]{1,0:T(8,128)S(1)}) custom-call(bf16[4,256,768]{2,1,0:T(8,128)(2,1)S(1)} %bitcast.87, bf16[256,768]{1,0:T(8,128)(2,1)S(1)} %copy-done.4, f32[256,768]{1,0:T(8,128)S(1)} %get-tuple-element.57.gr_ref, f32[8,768]{1,0:T(8,128)S(1)} %copy-done.19), custom_call_target="tpu_custom_call" | custom-call | tf_op jit(solution)/shard_map/last_step/pallas_call | solution.py:541
  240.7 13.2 %swap.1 = bf16[4,192,576]{2,1,0:T(8,128)(2,1)S(1)} custom-call(bf16[4,192,576]{2,1,0:T(8,128)(2,1)S(1)} %bitcast.85), custom_call_target="tpu_custom_call" | custom-call | tf_op jit(solution)/shard_map/swap/pallas_call | solution.py:349
  256.5 3.3 reshape.171
  259.8 36.1 %all-reduce.10.cloned.1.call-done = (bf16[192,768]{1,0:T(8,128)(2,1)}, bf16[192,3072]{1,0:T(8,128)(2,1)}) async-done(((bf16[192,768]{1,0:T(8,128)(2,1)}, bf16[192,3072]{1,0:T(8,128)(2,1)}), (bf16[192,768]{1,0:T(8,128)(2,1)}, bf16[192,3072]{1,0:T(8,128)(2,1)})) %all-reduce.10.cloned.1.call-update) | async-done | bytes 1474576 | tf_op jit(solution)/shard_map/psum | solution.py:717
  296.4 40.3 %psum.35 = f32[12,768]{1,0:T(8,128)S(1)} all-reduce(f32[12,768]{1,0:T(8,128)S(1)} %pad_maximum_fusion.3), channel_id=1, replica_groups=mesh['rep'=8,'cp'=4] {'rep','cp'}, use_global_device_ids=true, to_apply=%region_6.7 | all-reduce | flops 9216 | bytes 73728 | tf_op jit(solution)/shard_map/psum | solution.py:735
  338.8 3.0 convert_element_type.125
  346.3 59.7 %all-reduce.8.cloned.1.call-done = bf16[192,2304]{1,0:T(8,128)(2,1)} async-done(((bf16[192,2304]{1,0:T(8,128)(2,1)}), bf16[192,2304]{1,0:T(8,128)(2,1)}) %all-reduce.8.cloned.1.call-update) | async-done | bytes 884752 | tf_op jit(solution)/shard_map/psum | solution.py:723
  (212 shorter events, 73.9 us)
Async XLA Ops:
  7.2 107.5 %copy-start = (bf16[768,768]{1,0:T(8,128)(2,1)S(1)}, bf16[768,768]{1,0:T(8,128)(2,1)}, u32[]{:S(2)}) copy-start(bf16[768,768]{1,0:T(8,128)(2,1)} %param.26) | copy-start | bytes 3538948
  7.2 110.7 %all-gather.2.cloned.1.call-start = ((), (), s32[]{:S(2)}) async-start(), calls=%async_computation.1 | async-start | bytes 1966080 | tf_op jit(solution)/shard_map/all_gather | solution.py:677
  40.9 163.8 %all-reduce.6.cloned.1.call-start = ((), (), s32[]{:S(2)}) async-start(), calls=%async_computation.3 | async-start | bytes 2359296 | tf_op jit(solution)/shard_map/psum | solution.py:706
  51.1 56.2 %collective-permute-start = (bf16[1,192,768]{2,1,0:T(8,128)(2,1)}, bf16[1,192,768]{2,1,0:T(8,128)(2,1)}, u32[]{:S(2)}, u32[]{:S(2)}) collective-permute-start(bf16[1,192,768]{2,1,0:T(8,128)(2,1)} %bitcast.82), channel_id=1, source_target_pairs={{0,1},{1,2},{2,3},{3,0},{4,5},{5,6},{6,7},{7,4},{8,9},{9,10},{10,1... | collective-permute-start | bytes 884744 | tf_op jit(solution)/shard_map/ppermute | solution.py:655
  52.0 56.6 %collective-permute-start.1 = (bf16[1,192,768]{2,1,0:T(8,128)(2,1)}, bf16[1,192,768]{2,1,0:T(8,128)(2,1)}, u32[]{:S(2)}, u32[]{:S(2)}) collective-permute-start(bf16[1,192,768]{2,1,0:T(8,128)(2,1)} %bitcast.81), channel_id=1, source_target_pairs={{0,2},{1,3},{2,0},{3,1},{4,6},{5,7},{6,4},{7,5},{8,10},{9,11},{10,... | collective-permute-start | bytes 884744 | tf_op jit(solution)/shard_map/ppermute | solution.py:655
  54.3 55.2 %collective-permute-start.2 = (bf16[1,192,768]{2,1,0:T(8,128)(2,1)}, bf16[1,192,768]{2,1,0:T(8,128)(2,1)}, u32[]{:S(2)}, u32[]{:S(2)}) collective-permute-start(bf16[1,192,768]{2,1,0:T(8,128)(2,1)} %bitcast.80), channel_id=1, source_target_pairs={{0,3},{1,0},{2,1},{3,2},{4,7},{5,4},{6,5},{7,6},{8,11},{9,8},{10,9... | collective-permute-start | bytes 884744 | tf_op jit(solution)/shard_map/ppermute | solution.py:655
  85.7 21.5 %copy-start.33 = (bf16[4,192,768]{2,1,0:T(8,128)(2,1)S(1)}, bf16[4,192,768]{2,1,0:T(8,128)(2,1)}, u32[]{:S(2)}) copy-start(bf16[4,192,768]{2,1,0:T(8,128)(2,1)} %copy-done.32) | copy-start | bytes 3538948
  107.2 5.7 %copy-start.5 = (f32[256,768]{1,0:T(8,128)}, f32[256,768]{1,0:T(8,128)S(1)}, u32[]{:S(2)}) copy-start(f32[256,768]{1,0:T(8,128)S(1)} %get-tuple-element.46.r_ref) | copy-start | bytes 2359300
  123.2 172.6 %all-reduce.10.cloned.1.call-start = ((), (), s32[]{:S(2)}) async-start(), calls=%async_computation.5 | async-start | bytes 2949120 | tf_op jit(solution)/shard_map/psum | solution.py:717
  144.2 22.5 %copy-start.22 = (bf16[4,256,768]{2,1,0:T(8,128)(2,1)S(1)}, bf16[4,256,768]{2,1,0:T(8,128)(2,1)}, u32[]{:S(2)}) copy-start(bf16[4,256,768]{2,1,0:T(8,128)(2,1)} %copy-done.21) | copy-start | bytes 4718596
  168.4 7.4 %collective-permute-start.3 = (bf16[1,192,768]{2,1,0:T(8,128)(2,1)S(1)}, bf16[1,192,768]{2,1,0:T(8,128)(2,1)S(1)}, u32[]{:S(2)}, u32[]{:S(2)}) collective-permute-start(bf16[1,192,768]{2,1,0:T(8,128)(2,1)S(1)} %get-tuple-element.76), channel_id=1, source_target_pairs={{0,1},{1,2},{2,3},{3,0},{4,5},{5,6},{6,7},{7,4},{8,9},{9,10},{10,1... | collective-permute-start | bytes 884744 | tf_op jit(solution)/shard_map/ppermute | solution.py:655
  168.9 15.3 %collective-permute-start.5 = (bf16[1,192,768]{2,1,0:T(8,128)(2,1)S(1)}, bf16[1,192,768]{2,1,0:T(8,128)(2,1)S(1)}, u32[]{:S(2)}, u32[]{:S(2)}) collective-permute-start(bf16[1,192,768]{2,1,0:T(8,128)(2,1)S(1)} %get-tuple-element.74), channel_id=1, source_target_pairs={{0,3},{1,0},{2,1},{3,2},{4,7},{5,4},{6,5},{7,6},{8,11},{9,8},{10,9... | collective-permute-start | bytes 884744 | tf_op jit(solution)/shard_map/ppermute | solution.py:655
  170.2 13.9 %collective-permute-start.4 = (bf16[1,192,768]{2,1,0:T(8,128)(2,1)S(1)}, bf16[1,192,768]{2,1,0:T(8,128)(2,1)S(1)}, u32[]{:S(2)}, u32[]{:S(2)}) collective-permute-start(bf16[1,192,768]{2,1,0:T(8,128)(2,1)S(1)} %get-tuple-element.75), channel_id=1, source_target_pairs={{0,2},{1,3},{2,0},{3,1},{4,6},{5,7},{6,4},{7,5},{8,10},{9,11},{10,... | collective-permute-start | bytes 884744 | tf_op jit(solution)/shard_map/ppermute | solution.py:655
  185.4 20.0 %copy-start.42 = (f32[1,2,4,128]{3,2,1,0:T(4,128)S(1)}, f32[1,2,4,128]{3,2,1,0:T(4,128)}, u32[]{:S(2)}) copy-start(f32[1,2,4,128]{3,2,1,0:T(4,128)} %get-tuple-element.96) | copy-start | bytes 12292
  185.4 20.0 %copy-start.43 = (f32[1,2,4,128]{3,2,1,0:T(4,128)S(1)}, f32[1,2,4,128]{3,2,1,0:T(4,128)}, u32[]{:S(2)}) copy-start(f32[1,2,4,128]{3,2,1,0:T(4,128)} %get-tuple-element.98) | copy-start | bytes 12292
  185.4 20.0 %copy-start.41 = (f32[4,192]{1,0:T(4,128)S(1)}, f32[4,192]{1,0:T(4,128)}, u32[]{:S(2)}) copy-start(f32[4,192]{1,0:T(4,128)} %get-tuple-element.82) | copy-start | bytes 9220
  204.6 139.7 %reduce-scatter.2.cloned.1.call-start = ((), (), s32[]{:S(2)}) async-start(), calls=%async_computation.2 | async-start | bytes 1966080 | tf_op jit(solution)/shard_map/reduce_scatter | solution.py:710
  205.2 200.8 %all-reduce.8.cloned.1.call-start = ((), (), s32[]{:S(2)}) async-start(), calls=%async_computation.4 | async-start | bytes 1769472 | tf_op jit(solution)/shard_map/psum | solution.py:723
  214.8 9.5 %copy-start.25 = (bf16[4,192,576]{2,1,0:T(8,128)(2,1)S(1)}, bf16[4,192,576]{2,1,0:T(8,128)(2,1)}, u32[]{:S(2)}) copy-start(bf16[4,192,576]{2,1,0:T(8,128)(2,1)} %copy-done.23) | copy-start | bytes 2654212
  224.2 14.4 %copy-start.11 = (bf16[1024,192]{1,0:T(8,128)(2,1)}, bf16[1024,192]{1,0:T(8,128)(2,1)S(1)}, u32[]{:S(2)}) copy-start(bf16[1024,192]{1,0:T(8,128)(2,1)S(1)} %get-tuple-element.54) | copy-start | bytes 1179652
  225.7 12.9 %copy-start.30 = (bf16[1024,768]{1,0:T(8,128)(2,1)S(1)}, bf16[1024,768]{1,0:T(8,128)(2,1)}, u32[]{:S(2)}) copy-start(bf16[1024,768]{1,0:T(8,128)(2,1)} %fusion.10) | copy-start | bytes 4718596
  256.5 39.3 %copy-start.12 = (bf16[1024,192]{1,0:T(8,128)(2,1)S(1)}, bf16[1024,192]{1,0:T(8,128)(2,1)}, u32[]{:S(2)}) copy-start(bf16[1024,192]{1,0:T(8,128)(2,1)} %copy-done.11) | copy-start | bytes 1179652
  256.5 39.9 %copy-start.38 = (f32[4,768]{1,0:T(4,128)S(1)}, f32[4,768]{1,0:T(4,128)}, u32[]{:S(2)}) copy-start(f32[4,768]{1,0:T(4,128)} %slice.83) | copy-start | bytes 36868
  344.3 64.9 %copy-start.1 = (bf16[768,768]{1,0:T(8,128)(2,1)S(1)}, bf16[768,768]{1,0:T(8,128)(2,1)}, u32[]{:S(2)}) copy-start(bf16[768,768]{1,0:T(8,128)(2,1)} %param.26) | copy-start | bytes 3538948
  (40 other events, 79.0 us)
Sparse Core Ops, SparseCore 0:
  41.0 26.5 all-gather.1
  123.3 81.2 all-reduce.5
  209.5 86.3 all-reduce.9
  298.8 27.5 reduce-scatter.1
  330.1 75.8 all-reduce.7
